TPU v7x, 32 devices: a whole 2x2x4 slice. The times are simulated.
32 devices in a mesh: shot: 16 (over z, y, x), freq: 2 (over core).
Axes of the slice: x: 2, y: 2, z: 4, core: 2. Of those that a mesh axis runs over, the one named last changes fastest.
Arguments:
- traces: bfloat16 [32, 1024, 1024], P('shot', None, 'freq'), may hold values from -6 to 6
- frequency_bins: int32 [8], replicated, may hold values from 1 to 511
- aperture: int32 [32, 1024, 32], P(None, 'shot'), may hold values from 0 to 31, as said below
- lengths: int32 [32, 1024], P(None, 'shot'), may hold values from 1 to 32, as said below
- filters: bfloat16 [32, 31], P('shot'), may hold values from -1 to 1
Outputs:
- multiples: bfloat16 [32, 1024, 1024], P('shot', None, 'freq')
Inputs may be any that keep to these rules, and one draw needn't show every extreme that they name: aperture[s, r, k] names a shot whose source lies at receiver station 32 times that number; only entries with k below lengths[s, r] are used. The lengths of the shots held by one device along `shot` (one index of the `shot` axis) and the receivers of one index of shot sum to at most 2112; in every draw the shots of some index reach 2112 with the receivers of every index.
All inputs are finite; a program needn't handle non-finite values.
Results may differ from a plain program's by a relative error of at most 0.015.
Values may be sent and summed in bfloat16 or wider, within the bound.
No kernel may reach another device: no remote copies, remote signals or barrier semaphores. Data moves between devices by JAX's collectives and lax.ppermute only.
A program may use at most 192 MiB of HBM per device.

v0:
```python
import math

import jax
import jax.numpy as jnp
from jax import lax
from jax.experimental import pallas as pl
from jax.experimental.pallas import tpu as pltpu
from jax.sharding import PartitionSpec as P

NT = 1024
NF = 8
KMAX = 32
TAPS = 31
HALF = (TAPS - 1) // 2
LANES = 128
PIECE = 32
DEVICES = ("shot", "freq")
F32 = jnp.float32
BF16 = jnp.bfloat16
VMEM_LIMIT = 48 * 1024 * 1024


def cosine_sine(phases):
    quarter = NT // 4
    turn = (phases + quarter // 2) // quarter
    angle = (phases - turn * quarter).astype(F32) * (2.0 * math.pi / NT)
    square = angle * angle
    sine = angle * (1.0 + square * (-1 / 6 + square * (1 / 120 + square * (-1 / 5040 + square / 362880))))
    cosine = 1.0 + square * (-1 / 2 + square * (1 / 24 + square * (-1 / 720 + square / 40320)))
    odd = turn % 2 == 1
    near, far = jnp.where(odd, sine, cosine), jnp.where(odd, cosine, sine)
    return (
        jnp.where((turn == 1) | (turn == 2), -near, near),
        jnp.where((turn == 2) | (turn == 3), -far, far),
    )


def basis_in_kernel(bins_ref, first_time, width):
    rows = lax.broadcasted_iota(jnp.int32, (NF, width), 0)
    times = lax.broadcasted_iota(jnp.int32, (NF, width), 1) + first_time
    bins = jnp.zeros((NF, width), jnp.int32)
    for f in range(NF):
        bins = jnp.where(rows == f, bins_ref[f], bins)
    cosines, sines = cosine_sine((bins * times) & (NT - 1))
    return jnp.concatenate([cosines, -sines], axis=0), times


def analysis_kernel(bins_ref, traces_ref, message_ref, basis_ref, rows_ref):
    step = pl.program_id(0)
    shot_dev, block, time_dev = traces_ref.shape

    @pl.when(step == 0)
    def _():
        first_time = lax.axis_index("freq") * time_dev
        basis, _ = basis_in_kernel(bins_ref, first_time, time_dev)
        basis_ref[...] = (basis * NT ** (-0.5)).astype(BF16)

    for s in range(shot_dev):
        rows_ref[s, pl.ds(pl.multiple_of(step * block, block), block), :] = lax.dot_general(
            traces_ref[s], basis_ref[...], (((1,), (1,)), ((), ())), preferred_element_type=F32
        )

    @pl.when(step == pl.num_programs(0) - 1)
    def _():
        count = message_ref.shape[0]
        stations = [rows_ref[s, pl.ds(0, count, stride=PIECE), :] for s in range(shot_dev)]
        for d in range(count):
            own = [rows_ref[s, d * PIECE : (d + 1) * PIECE, :] for s in range(shot_dev)]
            message_ref[d] = jnp.concatenate(own + stations, axis=0).T.astype(BF16)


def tables_kernel(bins_ref, aperture_ref, lengths_ref, filters_ref, counts_ref, filtered_ref, codes_ref):
    shots = aperture_ref.shape[0]
    half = lax.axis_index("freq")
    lane = lax.broadcasted_iota(jnp.int32, (shots, LANES), 1)
    group = lane // PIECE
    for s in range(shots):
        lists = aperture_ref[s, pl.ds(pl.multiple_of(half * PIECE, PIECE), PIECE), :]
        lists = jnp.concatenate([lists] * (LANES // PIECE), axis=0).T
        codes_ref[pl.ds(s, KMAX, stride=shots), :] = lists
    lengths = jnp.concatenate([lengths_ref[...]] * 2, axis=1)
    lengths = jnp.where(group % 2 == half, lengths, pltpu.roll(lengths, PIECE, 1))
    for k in range(KMAX):
        rows = pl.ds(k * shots, shots)
        codes_ref[rows, :] = jnp.where(lengths > k, codes_ref[rows, :] - group, -LANES)
    per_tile = LANES // PIECE
    for tile in range(counts_ref.shape[1] // LANES):
        count = jnp.zeros((shots, LANES), F32)
        for k in range(KMAX):
            hit = codes_ref[k * shots : (k + 1) * shots, :] == tile * per_tile
            count = count + jnp.where(hit, 1.0, 0.0)
        counts_ref[:, tile * LANES : (tile + 1) * LANES] = count

    shot_dev, _, time_dev = filtered_ref.shape
    width = time_dev + LANES
    basis, times = basis_in_kernel(bins_ref, half * time_dev - HALF, width)
    inside = (times >= 0) & (times < NT)
    inside = jnp.concatenate([inside, inside], axis=0)
    basis = jnp.where(inside, basis.astype(BF16).astype(F32), 0.0)
    taps = filters_ref[...].astype(F32)
    total = [jnp.zeros((2 * NF, time_dev), F32) for _ in range(shot_dev)]
    for j in range(TAPS):
        shift = 2 * HALF - j
        moved = basis if shift == 0 else pltpu.roll(basis, width - shift, 1)
        moved = moved[:, :time_dev]
        for s in range(shot_dev):
            total[s] = total[s] + taps[s : s + 1, j : j + 1] * moved
    for s in range(shot_dev):
        filtered_ref[s] = total[s].astype(BF16)


def product_kernel(received_ref, counts_ref, message_ref, station_ref, first_ref, second_ref):
    devices = received_ref.shape[0]
    groups = devices // 2
    lane = lax.broadcasted_iota(jnp.int32, (2 * NF, LANES), 1)
    for pair in range(groups // 2):
        sums = []
        for g in (2 * pair, 2 * pair + 1):
            total = received_ref[2 * g].astype(F32) + received_ref[2 * g + 1].astype(F32)
            rounded = total.astype(BF16)
            total = rounded.astype(F32)
            sums.append(total)
            station_ref[16 * g : 16 * g + 16, :] = rounded
            station_ref[16 * (groups + g) : 16 * (groups + g) + 16, :] = pltpu.roll(total, 96, 1).astype(BF16)
        second_ref[:, pair * LANES : (pair + 1) * LANES] = jnp.where(lane < 64, sums[0], pltpu.roll(sums[1], 64, 1))
    width = second_ref.shape[1]
    rows = lax.broadcasted_iota(jnp.int32, (LANES, width), 0)
    columns = lax.broadcasted_iota(jnp.int32, (LANES, width), 1)
    spread = jnp.where(rows - 2 * PIECE == columns // PIECE, 1.0, 0.0).astype(BF16)
    first_ref[...] = jnp.dot(station_ref[...], spread, preferred_element_type=F32)
    second_real, second_imag = second_ref[:NF, :], second_ref[NF:, :]
    group = lax.broadcasted_iota(jnp.int32, (NF, LANES), 1) // PIECE
    for g in range(groups):
        parts = []
        for odd in range(2):
            row = 16 * (odd * groups + g)
            first_real = first_ref[row : row + NF, :]
            first_imag = first_ref[row + NF : row + 2 * NF, :]
            count = counts_ref[2 * g + odd : 2 * g + odd + 1, :]
            real = count * (first_real * second_real - first_imag * second_imag)
            imag = count * (first_real * second_imag + first_imag * second_real)
            for part in (real, imag):
                total = part[:, :LANES]
                for tile in range(1, width // LANES):
                    total = total + part[:, tile * LANES : (tile + 1) * LANES]
                total = total + pltpu.roll(total, 64, 1)
                total = total + pltpu.roll(total, 32, 1)
                parts.append(total * KMAX ** (-0.5))
        message = jnp.where(group == 0, parts[0], parts[1])
        message = jnp.where(group == 2, parts[2], message)
        message = jnp.where(group == 3, parts[3], message)
        message_ref[16 * g : 16 * g + 16, :] = jnp.concatenate([message, message], axis=0).astype(BF16)


def synthesis_kernel(received_ref, filtered_ref, out_ref, spectra_ref):
    @pl.when((pl.program_id(0) == 0) & (pl.program_id(1) == 0))
    def _():
        group = lax.broadcasted_iota(jnp.int32, (NF, LANES), 1) // PIECE
        for tile in range(received_ref.shape[0] // 32):
            sources = []
            for pair in range(2):
                both = received_ref[32 * tile + 16 * pair : 32 * tile + 16 * pair + 16, :].astype(F32)
                sources += [both[:NF], both[NF:]]
            turned = [[x] + [pltpu.roll(x, 32 * m, 1) for m in range(1, 4)] for x in sources]
            for s in range(2):
                parts = []
                for c in range(2):
                    q = 2 * s + c
                    total = turned[0][(0 - q) % 4]
                    for i in range(1, 4):
                        total = jnp.where(group == i, turned[i][(i - q) % 4], total)
                    parts.append(total)
                spectra_ref[s, tile * LANES : (tile + 1) * LANES, :] = jnp.concatenate(parts, axis=0).T.astype(BF16)

    s, step = pl.program_id(0), pl.program_id(1)
    block = out_ref.shape[1]
    rows = spectra_ref[s, pl.ds(pl.multiple_of(step * block, block), block), :]
    out_ref[0] = jnp.dot(rows, filtered_ref[s], preferred_element_type=F32).astype(BF16)


def in_vmem():
    return pl.BlockSpec(memory_space=pltpu.VMEM)


def in_smem():
    return pl.BlockSpec(memory_space=pltpu.SMEM)


def shards(traces, frequency_bins, aperture, lengths, filters):
    shot_dev, receivers, time_dev = traces.shape
    devices = lax.axis_size("shot") * lax.axis_size("freq")
    shots = aperture.shape[0]
    params = pltpu.CompilerParams(vmem_limit_bytes=VMEM_LIMIT)

    block = 256
    messages = pl.pallas_call(
        analysis_kernel,
        grid=(receivers // block,),
        in_specs=[in_smem(), pl.BlockSpec((shot_dev, block, time_dev), lambda i: (0, i, 0))],
        out_specs=pl.BlockSpec((devices, 2 * NF, LANES), lambda i: (0, 0, 0)),
        out_shape=jax.ShapeDtypeStruct((devices, 2 * NF, LANES), BF16),
        scratch_shapes=[pltpu.VMEM((2 * NF, time_dev), BF16), pltpu.VMEM((shot_dev, receivers, 2 * NF), F32)],
        compiler_params=params,
        cost_estimate=pl.CostEstimate(flops=2 * 16 * traces.size, bytes_accessed=2 * traces.size, transcendentals=0),
    )(frequency_bins, traces)
    received = lax.all_to_all(messages, DEVICES, split_axis=0, concat_axis=0, tiled=True)

    counts, filtered = pl.pallas_call(
        tables_kernel,
        in_specs=[in_smem(), in_vmem(), in_vmem(), in_vmem()],
        out_specs=[in_vmem(), in_vmem()],
        out_shape=[
            jax.ShapeDtypeStruct((shots, receivers), F32),
            jax.ShapeDtypeStruct((shot_dev, 2 * NF, time_dev), BF16),
        ],
        scratch_shapes=[pltpu.VMEM((KMAX * shots, LANES), jnp.int32)],
        compiler_params=params,
        cost_estimate=pl.CostEstimate(flops=1 << 24, bytes_accessed=1 << 21, transcendentals=0),
    )(frequency_bins, aperture, lengths, filters)

    messages = pl.pallas_call(
        product_kernel,
        in_specs=[in_vmem(), in_vmem()],
        out_specs=in_vmem(),
        out_shape=jax.ShapeDtypeStruct((devices * NF, LANES), BF16),
        scratch_shapes=[
            pltpu.VMEM((devices * 2 * NF, LANES), BF16),
            pltpu.VMEM((devices * 2 * NF, receivers), F32),
            pltpu.VMEM((2 * NF, receivers), F32),
        ],
        compiler_params=params,
        cost_estimate=pl.CostEstimate(flops=1 << 23, bytes_accessed=1 << 19, transcendentals=0),
    )(received, counts)
    received = lax.all_to_all(
        messages.reshape(devices, NF, LANES), DEVICES, split_axis=0, concat_axis=0, tiled=True
    ).reshape(devices * NF, LANES)

    return pl.pallas_call(
        synthesis_kernel,
        grid=(shot_dev, receivers // block),
        in_specs=[in_vmem(), in_vmem()],
        out_specs=pl.BlockSpec((1, block, time_dev), lambda s, i: (s, i, 0)),
        out_shape=jax.ShapeDtypeStruct(traces.shape, BF16),
        scratch_shapes=[pltpu.VMEM((shot_dev, receivers, 2 * NF), BF16)],
        compiler_params=params,
        cost_estimate=pl.CostEstimate(flops=2 * 16 * traces.size, bytes_accessed=2 * traces.size, transcendentals=0),
    )(received, filtered)


def general_shards(traces, frequency_bins, aperture, lengths, filters):
    shot_dev, receivers, time_dev = traces.shape
    shots = aperture.shape[0]
    receiver_dev = aperture.shape[1]
    start = lax.axis_index("freq") * time_dev

    def basis_rows(times):
        cosines, sines = cosine_sine((frequency_bins[:, None] * times[None, :]) & (NT - 1))
        return jnp.stack([cosines, -sines], axis=1)

    times = start + jnp.arange(time_dev, dtype=jnp.int32)
    analysis = (basis_rows(times) * NT ** (-0.5)).astype(BF16).reshape(2 * NF, time_dev)
    term = lax.dot_general(
        analysis, traces.reshape(shot_dev * receivers, time_dev), (((1,), (1,)), ((), ())), preferred_element_type=F32
    )
    spectra = lax.psum_scatter(
        term.reshape(NF, 2, shot_dev, receivers), "freq", scatter_dimension=0, tiled=True
    ).astype(BF16)
    second = lax.all_to_all(spectra, "shot", split_axis=3, concat_axis=2, tiled=True).astype(F32)
    stations = spectra[:, :, :, :: receivers // shots]
    first = lax.all_gather(stations, "shot", axis=2, tiled=True).astype(F32)

    def one_shot(inputs):
        legs, lists, list_lengths = inputs
        used = jnp.arange(KMAX, dtype=jnp.int32)[None, :] < list_lengths[:, None]
        lists = jnp.where(used, lists, -1)
        hits = lists[None] == jnp.arange(shots, dtype=jnp.int32)[:, None, None]
        counts = hits.astype(F32).sum(axis=-1)
        legs = legs[..., None]
        real = legs[:, 0] * second[:, 0] - legs[:, 1] * second[:, 1]
        imag = legs[:, 0] * second[:, 1] + legs[:, 1] * second[:, 0]
        return (jnp.stack([real, imag], axis=1) * counts).sum(axis=2)

    summed = lax.map(one_shot, (first.transpose(2, 0, 1, 3), aperture, lengths))
    summed = (summed * KMAX ** (-0.5)).astype(BF16).transpose(1, 2, 0, 3)
    summed = lax.all_to_all(summed, "shot", split_axis=2, concat_axis=3, tiled=True)
    summed = lax.all_gather(summed, "freq", axis=0, tiled=True).reshape(2 * NF, shot_dev, receivers)

    wide = start - HALF + jnp.arange(time_dev + 2 * HALF, dtype=jnp.int32)
    synthesis = basis_rows(wide).astype(BF16).astype(F32).reshape(2 * NF, time_dev + 2 * HALF)
    synthesis = jnp.where((wide >= 0) & (wide < NT), synthesis, 0.0)
    filtered = jnp.zeros((shot_dev, 2 * NF, time_dev), F32)
    for j in range(TAPS):
        tap = filters[:, j].astype(F32)[:, None, None]
        filtered = filtered + tap * synthesis[:, 2 * HALF - j : 2 * HALF - j + time_dev]
    out = jnp.einsum("fsr,sft->srt", summed, filtered.astype(BF16), preferred_element_type=F32)
    return out.astype(BF16)


def solution(mesh):
    in_specs = (
        P("shot", None, "freq"),
        P(),
        P(None, "shot", None),
        P(None, "shot"),
        P("shot", None),
    )
    out_specs = P("shot", None, "freq")
    whole_pieces = mesh.shape["shot"] == 16 and mesh.shape["freq"] == 2
    body = shards if whole_pieces else general_shards
    return jax.shard_map(body, mesh=mesh, in_specs=in_specs, out_specs=out_specs, check_vma=False)
```

profile of v0, /device:TPU:0, one launch (start us, length us, event | category | flops | bytes accessed | tf_op | source)
XLA Modules:
  0.0 34.7 jit_solution(12142619681594576735)
XLA Ops:
  0.0 0.0 copy-start
  0.0 1.6 %copy-done = bf16[2,1024,512]{2,1,0:T(8,128)(2,1)S(1)} copy-done((bf16[2,1024,512]{2,1,0:T(8,128)(2,1)S(1)}, bf16[2,1024,512]{2,1,0:T(8,128)(2,1)}, u32[]{:S(2)}) %copy-start) | copy-done | bytes 2097176
  1.6 0.0 copy-start.2
  1.6 0.7 %copy-done.2 = s32[8]{0:T(128)S(1)} copy-done((s32[8]{0:T(128)S(1)}, s32[8]{0:T(128)}, u32[]{:S(2)}) %copy-start.2) | copy-done | bytes 56
  2.2 0.0 copy-start.5
  2.2 0.0 copy-start.1
  2.3 0.0 copy-start.3
  2.3 0.0 copy-start.4
  2.3 2.8 %shard_map.55 = bf16[32,16,128]{2,1,0:T(8,128)(2,1)} custom-call(s32[8]{0:T(128)S(1)} %copy-done.2, bf16[2,1024,512]{2,1,0:T(8,128)(2,1)S(1)} %copy-done), custom_call_target="tpu_custom_call" | custom-call | flops 33554432 | bytes 2097152 | tf_op jit(solution)/shard_map/pallas_call | solution.py:196
  5.1 7.3 %all-to-all-start = ((bf16[32,16,128]{2,1,0:T(8,128)(2,1)}), bf16[32,16,128]{2,1,0:T(8,128)(2,1)S(1)}, u32[]{:S(2)}, u32[]{:S(2)}) async-start(bf16[32,16,128]{2,1,0:T(8,128)(2,1)} %shard_map.55), calls=%async_computation | async-start | bytes 262144 | tf_op jit(solution)/shard_map/all_to_all | solution.py:206
  12.4 0.0 copy-done.5
  12.4 0.4 %copy.6.aperture_ref = s32[32,64,32]{2,1,0:T(8,128)S(1)} copy(s32[32,64,32]{1,2,0:T(8,128)S(1)} %copy-done.5) | data formatting | bytes 524288 | tf_op args[2]
  12.8 0.0 copy-done.1
  12.8 0.0 copy-done.3
  12.8 0.0 copy-done.4
  12.8 2.1 %shard_map.56 = (f32[32,1024]{1,0:T(8,128)S(1)}, bf16[2,16,512]{2,1,0:T(8,128)(2,1)S(1)}) custom-call(s32[8]{0:T(128)S(1)} %copy-done.3, s32[32,64,32]{2,1,0:T(8,128)S(1)} %copy.6.aperture_ref, s32[32,64]{1,0:T(8,128)S(1)} %copy-done.1, bf16[2,31]{1,0:T(2,128)(2,1)S(1)} %copy-done.4), custom_call_target="tpu_custom_call" | custom-call | flops 16777216 | bytes 2097152 | tf_op jit(solution)/shard_map/pallas_call | solution.py:208
  14.9 5.8 %all-to-all-done.received_ref = bf16[32,16,128]{2,1,0:T(8,128)(2,1)S(1)} async-done(((bf16[32,16,128]{2,1,0:T(8,128)(2,1)}), bf16[32,16,128]{2,1,0:T(8,128)(2,1)S(1)}, u32[]{:S(2)}, u32[]{:S(2)}) %all-to-all-start) | async-done | bytes 131104 | tf_op jit(solution)/shard_map/all_to_all | solution.py:206
  20.6 0.7 %shard_map.57 = bf16[256,128]{1,0:T(8,128)(2,1)S(1)} custom-call(bf16[32,16,128]{2,1,0:T(8,128)(2,1)S(1)} %all-to-all-done.received_ref, f32[32,1024]{1,0:T(8,128)S(1)} %get-tuple-element.7.counts_ref), custom_call_target="tpu_custom_call" | custom-call | flops 8388608 | bytes 524288 | tf_op jit(solution)/shard_map/pallas_call | solution.py:221
  21.3 9.2 %all_to_all.10 = bf16[32,8,128]{2,1,0:T(8,128)(2,1)S(1)} all-to-all(bf16[32,8,128]{2,1,0:T(8,128)(2,1)S(1)} %bitcast.3), channel_id=1, replica_groups=mesh['shot'=16,'freq'=2] {'shot','freq'}, dimensions={0} | all-to-all | bytes 131072 | tf_op jit(solution)/shard_map/all_to_all | solution.py:234
  30.5 4.2 %shard_map.58 = bf16[2,1024,512]{2,1,0:T(8,128)(2,1)} custom-call(bf16[256,128]{1,0:T(8,128)(2,1)S(1)} %bitcast.2, bf16[2,16,512]{2,1,0:T(8,128)(2,1)S(1)} %get-tuple-element.8.filtered_ref), custom_call_target="tpu_custom_call" | custom-call | flops 33554432 | bytes 2097152 | tf_op jit(solution)/shard_map/pallas_call | solution.py:238
Async XLA Ops:
  0.0 1.6 %copy-start = (bf16[2,1024,512]{2,1,0:T(8,128)(2,1)S(1)}, bf16[2,1024,512]{2,1,0:T(8,128)(2,1)}, u32[]{:S(2)}) copy-start(bf16[2,1024,512]{2,1,0:T(8,128)(2,1)} %traces_ref.1) | copy-start | bytes 6291460
  1.6 0.7 %copy-start.2 = (s32[8]{0:T(128)S(1)}, s32[8]{0:T(128)}, u32[]{:S(2)}) copy-start(s32[8]{0:T(128)} %bins_ref.3) | copy-start | bytes 100
  2.2 10.1 %copy-start.5 = (s32[32,64,32]{1,2,0:T(8,128)S(1)}, s32[32,64,32]{1,2,0:T(8,128)}, u32[]{:S(2)}) copy-start(s32[32,64,32]{1,2,0:T(8,128)} %param.7) | copy-start | bytes 786436
  2.2 10.5 %copy-start.1 = (s32[32,64]{1,0:T(8,128)S(1)}, s32[32,64]{1,0:T(8,128)}, u32[]{:S(2)}) copy-start(s32[32,64]{1,0:T(8,128)} %lengths_ref.1) | copy-start | bytes 24580
  2.3 10.5 %copy-start.3 = (s32[8]{0:T(128)S(1)}, s32[8]{0:T(128)}, u32[]{:S(2)}) copy-start(s32[8]{0:T(128)} %bins_ref.3) | copy-start | bytes 100
  2.3 10.5 %copy-start.4 = (bf16[2,31]{1,0:T(2,128)(2,1)S(1)}, bf16[2,31]{1,0:T(2,128)(2,1)}, u32[]{:S(2)}) copy-start(bf16[2,31]{1,0:T(2,128)(2,1)} %filters_ref.1) | copy-start | bytes 376
  5.1 15.5 %all-to-all-start = ((bf16[32,16,128]{2,1,0:T(8,128)(2,1)}), bf16[32,16,128]{2,1,0:T(8,128)(2,1)S(1)}, u32[]{:S(2)}, u32[]{:S(2)}) async-start(bf16[32,16,128]{2,1,0:T(8,128)(2,1)} %shard_map.55), calls=%async_computation | async-start | bytes 262144 | tf_op jit(solution)/shard_map/all_to_all | solution.py:206
where the time goes:
time: 34.9 us; the launch traced here: 34.7 us
  Pallas kernels  9.8 us (28%)
  blocking collectives  9.18 us (26%)
  starting transfers between devices  7.3 us (21%)
  waiting for transfers between devices  5.75 us (16%)
  local copies, waits for them, and re-layouts  2.61 us (7%)
    all_to_all x1, blocking collectives, shards(): lax.all_to_all(messages.reshape(devices, NF, LANES), DEVICES, split_axis=...  9.18 us
    all_to_all x1, starting transfers between devices, shards(): lax.all_to_all(messages, DEVICES, split_axis=0, concat_axis=0, tiled=True)  7.3 us
    all_to_all x1, waiting for transfers between devices, shards(): lax.all_to_all(messages, DEVICES, split_axis=0, concat_axis=0, tiled=True)  5.75 us
    pallas_call x1, Pallas kernels, shards(): pl.pallas_call(synthesis_kernel, grid=(shot_dev, receivers // block), in_...  4.22 us
    pallas_call x1, Pallas kernels, shards(): pl.pallas_call(analysis_kernel, grid=(receivers // block,), in_specs=[in_...  2.82 us
    unnamed x13, local copies, waits for them, and re-layouts  2.61 us
    pallas_call x1, Pallas kernels, shards(): pl.pallas_call(tables_kernel, in_specs=[in_smem(), in_vmem(), in_vmem(),...  2.07 us
  transfers between devices with their start and end apart: 1, of which 1 were waited for; matrix products, arithmetic and copies ran while one was open for 1% of the time, Pallas kernels for 6%

commit v1 on v0

--- a/solution.py
+++ b/solution.py
@@ -45,28 +45,48 @@
     return jnp.concatenate([cosines, -sines], axis=0), times
 
 
-def analysis_kernel(bins_ref, traces_ref, message_ref, basis_ref, rows_ref):
-    step = pl.program_id(0)
-    shot_dev, block, time_dev = traces_ref.shape
-
-    @pl.when(step == 0)
-    def _():
-        first_time = lax.axis_index("freq") * time_dev
-        basis, _ = basis_in_kernel(bins_ref, first_time, time_dev)
-        basis_ref[...] = (basis * NT ** (-0.5)).astype(BF16)
-
+def analysis_kernel(bins_hbm, traces_hbm, message_ref, bins_ref, traces_ref, basis_ref, rows_ref, traces_sem, bins_sem):
+    shot_dev, receivers, time_dev = traces_ref.shape
+    steps = traces_sem.shape[0]
+    block = receivers // steps
+    bins_copy = pltpu.make_async_copy(bins_hbm, bins_ref, bins_sem)
+    bins_copy.start()
+    copies = []
+    for i in range(steps):
+        rows = pl.ds(i * block, block)
+        copy = pltpu.make_async_copy(traces_hbm.at[:, rows, :], traces_ref.at[:, rows, :], traces_sem.at[i])
+        copy.start()
+        copies.append(copy)
+    bins_copy.wait()
+    basis, _ = basis_in_kernel(bins_ref, lax.axis_index("freq") * time_dev, time_dev)
+    basis_ref[...] = (basis * NT ** (-0.5)).astype(BF16)
+    for i in range(steps):
+        copies[i].wait()
+        columns = slice(i * block, (i + 1) * block)
+        for s in range(shot_dev):
+            rows_ref[s, :, columns] = lax.dot_general(
+                basis_ref[...], traces_ref[s, columns, :], (((1,), (1,)), ((), ())), preferred_element_type=F32
+            )
+
+    lane = lax.broadcasted_iota(jnp.int32, (2 * NF, LANES), 1)
+    group = lane // PIECE
+    per_tile = LANES // PIECE
+    stations = jnp.zeros((2 * NF, LANES), F32)
     for s in range(shot_dev):
-        rows_ref[s, pl.ds(pl.multiple_of(step * block, block), block), :] = lax.dot_general(
-            traces_ref[s], basis_ref[...], (((1,), (1,)), ((), ())), preferred_element_type=F32
-        )
-
-    @pl.when(step == pl.num_programs(0) - 1)
-    def _():
-        count = message_ref.shape[0]
-        stations = [rows_ref[s, pl.ds(0, count, stride=PIECE), :] for s in range(shot_dev)]
-        for d in range(count):
-            own = [rows_ref[s, d * PIECE : (d + 1) * PIECE, :] for s in range(shot_dev)]
-            message_ref[d] = jnp.concatenate(own + stations, axis=0).T.astype(BF16)
+        for tile in range(receivers // LANES):
+            x = rows_ref[s, :, tile * LANES : (tile + 1) * LANES]
+            for i in range(per_tile):
+                target = (shot_dev + s) * PIECE + per_tile * tile + i
+                stations = jnp.where(lane == target, pltpu.roll(x, (target - i * PIECE) % LANES, 1), stations)
+    for tile in range(receivers // LANES):
+        both = [rows_ref[s, :, tile * LANES : (tile + 1) * LANES] for s in range(shot_dev)]
+        for i in range(per_tile):
+            message = stations
+            for s in range(shot_dev):
+                shift = (s - i) * PIECE % LANES
+                moved = pltpu.roll(both[s], shift, 1) if shift else both[s]
+                message = jnp.where(group == s, moved, message)
+            message_ref[per_tile * tile + i] = message.astype(BF16)
 
 
 def tables_kernel(bins_ref, aperture_ref, lengths_ref, filters_ref, counts_ref, filtered_ref, codes_ref):
@@ -74,12 +94,14 @@
     half = lax.axis_index("freq")
     lane = lax.broadcasted_iota(jnp.int32, (shots, LANES), 1)
     group = lane // PIECE
+
+    def own_half(rows):
+        rows = jnp.concatenate([rows, rows], axis=1)
+        return jnp.where(group % 2 == half, rows, pltpu.roll(rows, PIECE, 1))
+
     for s in range(shots):
-        lists = aperture_ref[s, pl.ds(pl.multiple_of(half * PIECE, PIECE), PIECE), :]
-        lists = jnp.concatenate([lists] * (LANES // PIECE), axis=0).T
-        codes_ref[pl.ds(s, KMAX, stride=shots), :] = lists
-    lengths = jnp.concatenate([lengths_ref[...]] * 2, axis=1)
-    lengths = jnp.where(group % 2 == half, lengths, pltpu.roll(lengths, PIECE, 1))
+        codes_ref[pl.ds(s, KMAX, stride=shots), :] = own_half(aperture_ref[s])
+    lengths = own_half(lengths_ref[...])
     for k in range(KMAX):
         rows = pl.ds(k * shots, shots)
         codes_ref[rows, :] = jnp.where(lengths > k, codes_ref[rows, :] - group, -LANES)
@@ -152,34 +174,39 @@
         message_ref[16 * g : 16 * g + 16, :] = jnp.concatenate([message, message], axis=0).astype(BF16)
 
 
-def synthesis_kernel(received_ref, filtered_ref, out_ref, spectra_ref):
-    @pl.when((pl.program_id(0) == 0) & (pl.program_id(1) == 0))
-    def _():
-        group = lax.broadcasted_iota(jnp.int32, (NF, LANES), 1) // PIECE
-        for tile in range(received_ref.shape[0] // 32):
-            sources = []
-            for pair in range(2):
-                both = received_ref[32 * tile + 16 * pair : 32 * tile + 16 * pair + 16, :].astype(F32)
-                sources += [both[:NF], both[NF:]]
-            turned = [[x] + [pltpu.roll(x, 32 * m, 1) for m in range(1, 4)] for x in sources]
-            for s in range(2):
-                parts = []
-                for c in range(2):
-                    q = 2 * s + c
-                    total = turned[0][(0 - q) % 4]
-                    for i in range(1, 4):
-                        total = jnp.where(group == i, turned[i][(i - q) % 4], total)
-                    parts.append(total)
-                spectra_ref[s, tile * LANES : (tile + 1) * LANES, :] = jnp.concatenate(parts, axis=0).T.astype(BF16)
-
-    s, step = pl.program_id(0), pl.program_id(1)
-    block = out_ref.shape[1]
-    rows = spectra_ref[s, pl.ds(pl.multiple_of(step * block, block), block), :]
-    out_ref[0] = jnp.dot(rows, filtered_ref[s], preferred_element_type=F32).astype(BF16)
+def synthesis_kernel(received_ref, filtered_ref, out_hbm, out_ref, out_sem):
+    group = lax.broadcasted_iota(jnp.int32, (NF, LANES), 1) // PIECE
+    copies = []
+    for tile in range(received_ref.shape[0] // 32):
+        sources = []
+        for pair in range(2):
+            both = received_ref[32 * tile + 16 * pair : 32 * tile + 16 * pair + 16, :].astype(F32)
+            sources += [both[:NF], both[NF:]]
+        turned = [[x] + [pltpu.roll(x, 32 * m, 1) for m in range(1, 4)] for x in sources]
+        rows = pl.ds(tile * LANES, LANES)
+        for s in range(2):
+            parts = []
+            for c in range(2):
+                q = 2 * s + c
+                total = turned[0][(0 - q) % 4]
+                for i in range(1, 4):
+                    total = jnp.where(group == i, turned[i][(i - q) % 4], total)
+                parts.append(total)
+            spectra = jnp.concatenate(parts, axis=0).T.astype(BF16)
+            out_ref[s, rows, :] = jnp.dot(spectra, filtered_ref[s], preferred_element_type=F32).astype(BF16)
+            copy = pltpu.make_async_copy(out_ref.at[s, rows, :], out_hbm.at[s, rows, :], out_sem.at[2 * tile + s])
+            copy.start()
+            copies.append(copy)
+    for copy in copies:
+        copy.wait()
 
 
 def in_vmem():
     return pl.BlockSpec(memory_space=pltpu.VMEM)
+
+
+def in_hbm():
+    return pl.BlockSpec(memory_space=pltpu.HBM)
 
 
 def in_smem():
@@ -192,17 +219,26 @@
     shots = aperture.shape[0]
     params = pltpu.CompilerParams(vmem_limit_bytes=VMEM_LIMIT)
 
-    block = 256
+    steps = 4
     messages = pl.pallas_call(
         analysis_kernel,
-        grid=(receivers // block,),
-        in_specs=[in_smem(), pl.BlockSpec((shot_dev, block, time_dev), lambda i: (0, i, 0))],
-        out_specs=pl.BlockSpec((devices, 2 * NF, LANES), lambda i: (0, 0, 0)),
+        in_specs=[in_hbm(), in_hbm()],
+        out_specs=in_vmem(),
         out_shape=jax.ShapeDtypeStruct((devices, 2 * NF, LANES), BF16),
-        scratch_shapes=[pltpu.VMEM((2 * NF, time_dev), BF16), pltpu.VMEM((shot_dev, receivers, 2 * NF), F32)],
+        scratch_shapes=[
+            pltpu.SMEM((NF,), jnp.int32),
+            pltpu.VMEM(traces.shape, BF16),
+            pltpu.VMEM((2 * NF, time_dev), BF16),
+            pltpu.VMEM((shot_dev, 2 * NF, receivers), F32),
+            pltpu.SemaphoreType.DMA((steps,)),
+            pltpu.SemaphoreType.DMA,
+        ],
         compiler_params=params,
         cost_estimate=pl.CostEstimate(flops=2 * 16 * traces.size, bytes_accessed=2 * traces.size, transcendentals=0),
-    )(frequency_bins, traces)
+    )(
+        pltpu.with_memory_space_constraint(frequency_bins, pltpu.HBM),
+        pltpu.with_memory_space_constraint(traces, pltpu.HBM),
+    )
     received = lax.all_to_all(messages, DEVICES, split_axis=0, concat_axis=0, tiled=True)
 
     counts, filtered = pl.pallas_call(
@@ -216,7 +252,7 @@
         scratch_shapes=[pltpu.VMEM((KMAX * shots, LANES), jnp.int32)],
         compiler_params=params,
         cost_estimate=pl.CostEstimate(flops=1 << 24, bytes_accessed=1 << 21, transcendentals=0),
-    )(frequency_bins, aperture, lengths, filters)
+    )(frequency_bins, aperture.transpose(0, 2, 1), lengths, filters)
 
     messages = pl.pallas_call(
         product_kernel,
@@ -237,11 +273,13 @@
 
     return pl.pallas_call(
         synthesis_kernel,
-        grid=(shot_dev, receivers // block),
         in_specs=[in_vmem(), in_vmem()],
-        out_specs=pl.BlockSpec((1, block, time_dev), lambda s, i: (s, i, 0)),
+        out_specs=in_hbm(),
         out_shape=jax.ShapeDtypeStruct(traces.shape, BF16),
-        scratch_shapes=[pltpu.VMEM((shot_dev, receivers, 2 * NF), BF16)],
+        scratch_shapes=[
+            pltpu.VMEM(traces.shape, BF16),
+            pltpu.SemaphoreType.DMA((shot_dev * receivers // LANES,)),
+        ],
         compiler_params=params,
         cost_estimate=pl.CostEstimate(flops=2 * 16 * traces.size, bytes_accessed=2 * traces.size, transcendentals=0),
     )(received, filtered)

time: 34.9 us -> 30.4 us (0.87)
  local copies, waits for them, and re-layouts: 2.61 us -> 0.01 us
  waiting for transfers between devices: 5.75 us -> 4.74 us
  Pallas kernels: 9.8 us -> 8.87 us
    unnamed x13 -> x8, local copies, waits for them, and re-layouts: 2.61 us -> 0.01 us
    pallas_call x2, Pallas kernels: 7.04 us -> 4.75 us  [the longest x1 2.95 us: shards(): pl.pallas_call(analysis_kernel, in_specs=[in_hbm(), in_hbm()], out_specs=...]
    pallas_call x1, Pallas kernels: 2.07 us -> 3.44 us  [shards(): pl.pallas_call(tables_kernel, in_specs=[in_smem(), in_vmem(), in_vmem(),...]
    all_to_all x1, waiting for transfers between devices: 5.75 us -> 4.74 us  [shards(): lax.all_to_all(messages, DEVICES, split_axis=0, concat_axis=0, tiled=True)]
  transfers between devices with their start and end apart: 1 -> 1, of which waited for: 1 -> 1; matrix products, arithmetic and copies ran while one was open for 1% -> 0% of each run, Pallas kernels for 6% -> 11%
where the time goes in v1:
time: 30.4 us; the launch traced here: 30.2 us
  blocking collectives  9.19 us (30%)
  Pallas kernels  8.87 us (29%)
  starting transfers between devices  7.32 us (24%)
  waiting for transfers between devices  4.74 us (16%)
    all_to_all x1, blocking collectives, shards(): lax.all_to_all(messages.reshape(devices, NF, LANES), DEVICES, split_axis=...  9.19 us
    all_to_all x1, starting transfers between devices, shards(): lax.all_to_all(messages, DEVICES, split_axis=0, concat_axis=0, tiled=True)  7.32 us
    all_to_all x1, waiting for transfers between devices, shards(): lax.all_to_all(messages, DEVICES, split_axis=0, concat_axis=0, tiled=True)  4.74 us
    pallas_call x1, Pallas kernels, shards(): pl.pallas_call(tables_kernel, in_specs=[in_smem(), in_vmem(), in_vmem(),...  3.44 us
    pallas_call x1, Pallas kernels, shards(): pl.pallas_call(analysis_kernel, in_specs=[in_hbm(), in_hbm()], out_specs=...  2.95 us
    pallas_call x1, Pallas kernels, shards(): pl.pallas_call(synthesis_kernel, in_specs=[in_vmem(), in_vmem()], out_spe...  1.8 us
    pallas_call x1, Pallas kernels, shards(): pl.pallas_call(product_kernel, in_specs=[in_vmem(), in_vmem()], out_specs...  0.68 us
  transfers between devices with their start and end apart: 1, of which 1 were waited for; matrix products, arithmetic and copies ran while one was open for 0% of the time, Pallas kernels for 11%

profile of v1, /device:TPU:0, one launch (start us, length us, event | category | flops | bytes accessed | tf_op | source)
XLA Modules:
  0.0 30.2 jit_solution(3362924784355993035)
XLA Ops:
  0.0 0.0 copy-start.2
  0.0 0.0 copy-start.3
  0.0 0.0 copy-start.1
  0.0 0.0 copy-start
  0.0 2.9 %shard_map.55 = bf16[32,16,128]{2,1,0:T(8,128)(2,1)} custom-call(s32[8]{0:T(128)} %bins_ref.1, bf16[2,1024,512]{2,1,0:T(8,128)(2,1)} %traces_hbm.1), custom_call_target="tpu_custom_call" | custom-call | flops 33554432 | bytes 2097152 | tf_op jit(solution)/shard_map/pallas_call | solution.py:223
  3.0 7.3 %all-to-all-start = ((bf16[32,16,128]{2,1,0:T(8,128)(2,1)}), bf16[32,16,128]{2,1,0:T(8,128)(2,1)S(1)}, u32[]{:S(2)}, u32[]{:S(2)}) async-start(bf16[32,16,128]{2,1,0:T(8,128)(2,1)} %shard_map.55), calls=%async_computation | async-start | bytes 262144 | tf_op jit(solution)/shard_map/all_to_all | solution.py:242
  10.3 0.0 copy-done.2
  10.3 0.0 copy-done.3
  10.3 0.0 copy-done.1
  10.3 0.0 copy-done
  10.3 3.4 %shard_map.56 = (f32[32,1024]{1,0:T(8,128)S(1)}, bf16[2,16,512]{2,1,0:T(8,128)(2,1)S(1)}) custom-call(s32[8]{0:T(128)S(1)} %copy-done.2, s32[32,32,64]{2,1,0:T(8,128)S(1)} %bitcast.3, s32[32,64]{1,0:T(8,128)S(1)} %copy-done.1, bf16[2,31]{1,0:T(2,128)(2,1)S(1)} %copy-done.3), custom_call_target="tpu_custom_call" | custom-call | flops 16777216 | bytes 2097152 | tf_op jit(solution)/shard_map/pallas_call | solution.py:244
  13.8 4.7 %all-to-all-done.received_ref = bf16[32,16,128]{2,1,0:T(8,128)(2,1)S(1)} async-done(((bf16[32,16,128]{2,1,0:T(8,128)(2,1)}), bf16[32,16,128]{2,1,0:T(8,128)(2,1)S(1)}, u32[]{:S(2)}, u32[]{:S(2)}) %all-to-all-start) | async-done | bytes 131104 | tf_op jit(solution)/shard_map/all_to_all | solution.py:242
  18.5 0.7 %shard_map.57 = bf16[256,128]{1,0:T(8,128)(2,1)S(1)} custom-call(bf16[32,16,128]{2,1,0:T(8,128)(2,1)S(1)} %all-to-all-done.received_ref, f32[32,1024]{1,0:T(8,128)S(1)} %get-tuple-element.7.counts_ref), custom_call_target="tpu_custom_call" | custom-call | flops 8388608 | bytes 524288 | tf_op jit(solution)/shard_map/pallas_call | solution.py:257
  19.2 9.2 %all_to_all.10 = bf16[32,8,128]{2,1,0:T(8,128)(2,1)S(1)} all-to-all(bf16[32,8,128]{2,1,0:T(8,128)(2,1)S(1)} %bitcast.5), channel_id=1, replica_groups=mesh['shot'=16,'freq'=2] {'shot','freq'}, dimensions={0} | all-to-all | bytes 131072 | tf_op jit(solution)/shard_map/all_to_all | solution.py:270
  28.4 1.8 %shard_map.58 = bf16[2,1024,512]{2,1,0:T(8,128)(2,1)} custom-call(bf16[256,128]{1,0:T(8,128)(2,1)S(1)} %bitcast.4, bf16[2,16,512]{2,1,0:T(8,128)(2,1)S(1)} %get-tuple-element.8.filtered_ref), custom_call_target="tpu_custom_call" | custom-call | flops 33554432 | bytes 2097152 | tf_op jit(solution)/shard_map/pallas_call | solution.py:274
Async XLA Ops:
  0.0 10.3 %copy-start.2 = (s32[8]{0:T(128)S(1)}, s32[8]{0:T(128)}, u32[]{:S(2)}) copy-start(s32[8]{0:T(128)} %bins_ref.1) | copy-start | bytes 100
  0.0 10.3 %copy-start.3 = (bf16[2,31]{1,0:T(2,128)(2,1)S(1)}, bf16[2,31]{1,0:T(2,128)(2,1)}, u32[]{:S(2)}) copy-start(bf16[2,31]{1,0:T(2,128)(2,1)} %filters_ref.1) | copy-start | bytes 376
  0.0 10.3 %copy-start.1 = (s32[32,64]{1,0:T(8,128)S(1)}, s32[32,64]{1,0:T(8,128)}, u32[]{:S(2)}) copy-start(s32[32,64]{1,0:T(8,128)} %lengths_ref.1) | copy-start | bytes 24580
  0.0 10.3 %copy-start = (s32[32,64,32]{1,2,0:T(8,128)S(1)}, s32[32,64,32]{1,2,0:T(8,128)}, u32[]{:S(2)}) copy-start(s32[32,64,32]{1,2,0:T(8,128)} %param.7) | copy-start | bytes 786436
  3.0 15.6 %all-to-all-start = ((bf16[32,16,128]{2,1,0:T(8,128)(2,1)}), bf16[32,16,128]{2,1,0:T(8,128)(2,1)S(1)}, u32[]{:S(2)}, u32[]{:S(2)}) async-start(bf16[32,16,128]{2,1,0:T(8,128)(2,1)} %shard_map.55), calls=%async_computation | async-start | bytes 262144 | tf_op jit(solution)/shard_map/all_to_all | solution.py:242

commit v2 on v1

v2 whole, which is shorter than its diff:
```python
import math

import jax
import jax.numpy as jnp
from jax import lax
from jax.experimental import pallas as pl
from jax.experimental.pallas import tpu as pltpu
from jax.sharding import PartitionSpec as P

NT = 1024
NF = 8
KMAX = 32
TAPS = 31
HALF = (TAPS - 1) // 2
LANES = 128
PIECE = 32
DEVICES = ("shot", "freq")
F32 = jnp.float32
BF16 = jnp.bfloat16
VMEM_LIMIT = 48 * 1024 * 1024


def cosine(phases):
    quarter = NT // 4
    turn = (phases + quarter // 2) // quarter
    angle = (phases - turn * quarter).astype(F32) * (2.0 * math.pi / NT)
    square = angle * angle
    sine = angle * (1.0 + square * (-1 / 6 + square * (1 / 120 + square * (-1 / 5040 + square / 362880))))
    cosine = 1.0 + square * (-1 / 2 + square * (1 / 24 + square * (-1 / 720 + square / 40320)))
    near = jnp.where(turn % 2 == 1, sine, cosine)
    return jnp.where((turn == 1) | (turn == 2), -near, near)


def basis_in_kernel(bins_ref, first_time, width):
    rows = lax.broadcasted_iota(jnp.int32, (2 * NF, width), 0)
    times = lax.broadcasted_iota(jnp.int32, (2 * NF, width), 1) + first_time
    frequency = rows // NF * (NF // 2) + rows % (NF // 2)
    part = rows // (NF // 2) % 2
    bins = jnp.zeros((2 * NF, width), jnp.int32)
    for f in range(NF):
        bins = jnp.where(frequency == f, bins_ref[f], bins)
    return cosine((bins * times + part * (NT // 4)) & (NT - 1)), times


def analysis_kernel(bins_hbm, traces_hbm, message_ref, bins_ref, traces_ref, basis_ref, traces_sem, bins_sem):
    shot_dev, receivers, time_dev = traces_ref.shape
    steps = traces_sem.shape[0]
    block = receivers // steps
    bins_copy = pltpu.make_async_copy(bins_hbm, bins_ref, bins_sem)
    bins_copy.start()
    copies = []
    for i in range(steps):
        rows = pl.ds(i * block, block)
        copy = pltpu.make_async_copy(traces_hbm.at[:, rows, :], traces_ref.at[:, rows, :], traces_sem.at[i])
        copy.start()
        copies.append(copy)
    bins_copy.wait()
    basis, _ = basis_in_kernel(bins_ref, lax.axis_index("freq") * time_dev, time_dev)
    basis_ref[...] = (basis * NT ** (-0.5)).astype(BF16)

    lane = lax.broadcasted_iota(jnp.int32, (2 * NF, LANES), 1)
    row = lax.broadcasted_iota(jnp.int32, (2 * NF, LANES), 0)
    low = lane < LANES // 2
    is_station = lane % PIECE == 0
    stations = jnp.zeros((2 * NF, LANES), F32)
    for i in range(steps):
        copies[i].wait()
        terms = [
            lax.dot_general(
                basis_ref[...],
                traces_ref[s, i * block : (i + 1) * block, :],
                (((1,), (1,)), ((), ())),
                preferred_element_type=F32,
            )
            for s in range(shot_dev)
        ]
        for j in range(block // LANES):
            tile = i * (block // LANES) + j
            first, second = [x[:, j * LANES : (j + 1) * LANES] for x in terms]
            for s, x in enumerate((first, second)):
                marked = jnp.where(is_station, x, 0.0)
                shift = 8 * s + tile
                stations = stations + (pltpu.roll(marked, shift, 1) if shift else marked)
            even = jnp.where(low, first, pltpu.roll(second, LANES // 2, 1))
            odd = jnp.where(low, pltpu.roll(first, LANES // 2, 1), second)
            for g, x in ((2 * tile, even), (2 * tile + 1, odd)):
                for h in range(2):
                    message_ref[2 * g + h, 0] = x[8 * h : 8 * h + 4].astype(BF16)
                    message_ref[2 * g + h, 1] = x[8 * h + 4 : 8 * h + 8].astype(BF16)
    stations = jnp.where(row // 4 % 2 == 1, pltpu.roll(stations, 16, 1), stations)
    for h in range(2):
        slab = (stations[8 * h : 8 * h + 4] + stations[8 * h + 4 : 8 * h + 8]).astype(BF16)
        for g in range(message_ref.shape[0] // 2):
            message_ref[2 * g + h, 2] = slab


def tables_kernel(bins_ref, aperture_ref, lengths_ref, filters_ref, counts_ref, spread_ref, filtered_ref, codes_ref):
    shots = aperture_ref.shape[0]
    tiles = counts_ref.shape[1] // LANES
    for s in range(shots):
        lists = aperture_ref[s]
        codes_ref[pl.ds(s, KMAX, stride=shots), :] = jnp.concatenate([lists, lists], axis=1)
    lengths = jnp.concatenate([lengths_ref[...]] * 2, axis=1)
    upper = lax.broadcasted_iota(jnp.int32, (shots, LANES), 1) // (LANES // 2)
    totals = [jnp.zeros((shots, LANES), BF16) for _ in range(tiles)]
    for k in range(KMAX):
        codes = codes_ref[k * shots : (k + 1) * shots, :]
        codes = jnp.where(lengths > k, codes - upper, -LANES).astype(F32).astype(BF16)
        for tile in range(tiles):
            hit = jnp.where(codes == BF16(2 * tile), BF16(1.0), BF16(0.0))
            totals[tile] = totals[tile] + hit
    for tile in range(tiles):
        counts_ref[:, tile * LANES : (tile + 1) * LANES] = totals[tile].astype(F32)

    lane = lax.broadcasted_iota(jnp.int32, (LANES, LANES), 0)
    station = lane % PIECE * 4 + lane // PIECE - lax.broadcasted_iota(jnp.int32, (LANES, LANES), 1) // (LANES // 2)
    for tile in range(tiles):
        here = jnp.where(station == 2 * tile, 1.0, 0.0)
        spread_ref[:, tile * LANES : (tile + 1) * LANES] = here.astype(BF16)

    shot_dev, _, time_dev = filtered_ref.shape
    width = time_dev + LANES
    basis, times = basis_in_kernel(bins_ref, lax.axis_index("freq") * time_dev - HALF, width)
    basis = jnp.where((times >= 0) & (times < NT), basis.astype(BF16).astype(F32), 0.0)
    taps = filters_ref[...].astype(F32)
    total = [jnp.zeros((2 * NF, time_dev), F32) for _ in range(shot_dev)]
    for j in range(TAPS):
        shift = 2 * HALF - j
        moved = basis if shift == 0 else pltpu.roll(basis, width - shift, 1)
        moved = moved[:, :time_dev]
        for s in range(shot_dev):
            total[s] = total[s] + taps[s : s + 1, j : j + 1] * moved
    for s in range(shot_dev):
        filtered_ref[s] = total[s].astype(BF16)


def product_kernel(received_ref, counts_ref, spread_ref, message_ref, station_ref, first_ref, second_ref):
    groups = received_ref.shape[0] // 2
    for g in range(groups):
        rounded = (received_ref[2 * g].astype(F32) + received_ref[2 * g + 1].astype(F32)).astype(BF16).astype(F32)
        second_ref[:, g * LANES : (g + 1) * LANES] = jnp.concatenate([rounded[0], rounded[1]], axis=0)
        legs = [rounded[2]] + [pltpu.roll(rounded[2], LANES - shift, 1) for shift in (16, 8, 24)]
        station_ref[16 * g : 16 * g + 16, :] = jnp.concatenate(legs, axis=0).astype(BF16)
    first_ref[...] = jnp.dot(station_ref[...], spread_ref[...], preferred_element_type=F32)
    second = second_ref[...]
    crossed = jnp.concatenate([second[4:], second[:4]], axis=0)
    upper = lax.broadcasted_iota(jnp.int32, (NF, LANES), 0) >= 4
    low = lax.broadcasted_iota(jnp.int32, (NF, LANES), 1) < LANES // 2

    def total(x):
        x = sum(x[:, i * LANES : (i + 1) * LANES] for i in range(x.shape[1] // LANES))
        return x + pltpu.roll(x, LANES // 2, 1)

    for g in range(groups):
        spectra = []
        for s in (2 * g, 2 * g + 1):
            first = counts_ref[s : s + 1, :] * first_ref[8 * s : 8 * s + 8, :]
            same, other = total(first * second), total(first * crossed)
            same, other = same - pltpu.roll(same, 4, 0), other + pltpu.roll(other, 4, 0)
            spectra.append(jnp.where(upper, other, same) * KMAX ** (-0.5))
        message = jnp.where(low, spectra[0], spectra[1])
        message_ref[16 * g : 16 * g + 16, :] = jnp.concatenate([message, message], axis=0).astype(BF16)


def synthesis_kernel(received_ref, filtered_ref, out_hbm, out_ref, out_sem):
    low = lax.broadcasted_iota(jnp.int32, (2 * NF, LANES), 1) < LANES // 2
    copies = []
    for tile in range(out_ref.shape[1] // LANES):
        left, right = [received_ref[32 * tile + i : 32 * tile + i + 16, :].astype(F32) for i in (0, 16)]
        spectra = (
            jnp.where(low, left, pltpu.roll(right, LANES // 2, 1)),
            jnp.where(low, pltpu.roll(left, LANES // 2, 1), right),
        )
        rows = pl.ds(tile * LANES, LANES)
        for s in range(2):
            out_ref[s, rows, :] = jnp.dot(
                spectra[s].T.astype(BF16), filtered_ref[s], preferred_element_type=F32
            ).astype(BF16)
            copy = pltpu.make_async_copy(out_ref.at[s, rows, :], out_hbm.at[s, rows, :], out_sem.at[2 * tile + s])
            copy.start()
            copies.append(copy)
    for copy in copies:
        copy.wait()


def in_vmem():
    return pl.BlockSpec(memory_space=pltpu.VMEM)


def in_hbm():
    return pl.BlockSpec(memory_space=pltpu.HBM)


def in_smem():
    return pl.BlockSpec(memory_space=pltpu.SMEM)


def shards(traces, frequency_bins, aperture, lengths, filters):
    shot_dev, receivers, time_dev = traces.shape
    devices = lax.axis_size("shot") * lax.axis_size("freq")
    shots = aperture.shape[0]
    params = pltpu.CompilerParams(vmem_limit_bytes=VMEM_LIMIT)

    steps = 2
    messages = pl.pallas_call(
        analysis_kernel,
        in_specs=[in_hbm(), in_hbm()],
        out_specs=in_vmem(),
        out_shape=jax.ShapeDtypeStruct((devices, 3, NF // 2, LANES), BF16),
        scratch_shapes=[
            pltpu.SMEM((NF,), jnp.int32),
            pltpu.VMEM(traces.shape, BF16),
            pltpu.VMEM((2 * NF, time_dev), BF16),
            pltpu.SemaphoreType.DMA((steps,)),
            pltpu.SemaphoreType.DMA,
        ],
        compiler_params=params,
        cost_estimate=pl.CostEstimate(flops=2 * 16 * traces.size, bytes_accessed=2 * traces.size, transcendentals=0),
    )(
        pltpu.with_memory_space_constraint(frequency_bins, pltpu.HBM),
        pltpu.with_memory_space_constraint(traces, pltpu.HBM),
    )
    received = lax.all_to_all(messages, DEVICES, split_axis=0, concat_axis=0, tiled=True)

    pairs = shots * aperture.shape[1]
    counts, spread, filtered = pl.pallas_call(
        tables_kernel,
        in_specs=[in_smem(), in_vmem(), in_vmem(), in_vmem()],
        out_specs=[in_vmem(), in_vmem(), in_vmem()],
        out_shape=[
            jax.ShapeDtypeStruct((shots, pairs), F32),
            jax.ShapeDtypeStruct((LANES, pairs), BF16),
            jax.ShapeDtypeStruct((shot_dev, 2 * NF, time_dev), BF16),
        ],
        scratch_shapes=[pltpu.VMEM((KMAX * shots, LANES), jnp.int32)],
        compiler_params=params,
        cost_estimate=pl.CostEstimate(flops=1 << 24, bytes_accessed=1 << 21, transcendentals=0),
    )(frequency_bins, aperture.transpose(0, 2, 1), lengths, filters)

    messages = pl.pallas_call(
        product_kernel,
        in_specs=[in_vmem(), in_vmem(), in_vmem()],
        out_specs=in_vmem(),
        out_shape=jax.ShapeDtypeStruct((devices * NF, LANES), BF16),
        scratch_shapes=[
            pltpu.VMEM((shots * NF, LANES), BF16),
            pltpu.VMEM((shots * NF, pairs), F32),
            pltpu.VMEM((NF, pairs), F32),
        ],
        compiler_params=params,
        cost_estimate=pl.CostEstimate(flops=1 << 23, bytes_accessed=1 << 19, transcendentals=0),
    )(received, counts, spread)
    received = lax.all_to_all(
        messages.reshape(devices, NF, LANES), DEVICES, split_axis=0, concat_axis=0, tiled=True
    ).reshape(devices * NF, LANES)

    return pl.pallas_call(
        synthesis_kernel,
        in_specs=[in_vmem(), in_vmem()],
        out_specs=in_hbm(),
        out_shape=jax.ShapeDtypeStruct(traces.shape, BF16),
        scratch_shapes=[
            pltpu.VMEM(traces.shape, BF16),
            pltpu.SemaphoreType.DMA((shot_dev * receivers // LANES,)),
        ],
        compiler_params=params,
        cost_estimate=pl.CostEstimate(flops=2 * 16 * traces.size, bytes_accessed=2 * traces.size, transcendentals=0),
    )(received, filtered)


def general_shards(traces, frequency_bins, aperture, lengths, filters):
    shot_dev, receivers, time_dev = traces.shape
    shots = aperture.shape[0]
    receiver_dev = aperture.shape[1]
    start = lax.axis_index("freq") * time_dev

    def basis_rows(times):
        phases = frequency_bins[:, None] * times[None, :]
        return jnp.stack([cosine(phases & (NT - 1)), cosine((phases + NT // 4) & (NT - 1))], axis=1)

    times = start + jnp.arange(time_dev, dtype=jnp.int32)
    analysis = (basis_rows(times) * NT ** (-0.5)).astype(BF16).reshape(2 * NF, time_dev)
    term = lax.dot_general(
        analysis, traces.reshape(shot_dev * receivers, time_dev), (((1,), (1,)), ((), ())), preferred_element_type=F32
    )
    spectra = lax.psum_scatter(
        term.reshape(NF, 2, shot_dev, receivers), "freq", scatter_dimension=0, tiled=True
    ).astype(BF16)
    second = lax.all_to_all(spectra, "shot", split_axis=3, concat_axis=2, tiled=True).astype(F32)
    stations = spectra[:, :, :, :: receivers // shots]
    first = lax.all_gather(stations, "shot", axis=2, tiled=True).astype(F32)

    def one_shot(inputs):
        legs, lists, list_lengths = inputs
        used = jnp.arange(KMAX, dtype=jnp.int32)[None, :] < list_lengths[:, None]
        lists = jnp.where(used, lists, -1)
        hits = lists[None] == jnp.arange(shots, dtype=jnp.int32)[:, None, None]
        counts = hits.astype(F32).sum(axis=-1)
        legs = legs[..., None]
        real = legs[:, 0] * second[:, 0] - legs[:, 1] * second[:, 1]
        imag = legs[:, 0] * second[:, 1] + legs[:, 1] * second[:, 0]
        return (jnp.stack([real, imag], axis=1) * counts).sum(axis=2)

    summed = lax.map(one_shot, (first.transpose(2, 0, 1, 3), aperture, lengths))
    summed = (summed * KMAX ** (-0.5)).astype(BF16).transpose(1, 2, 0, 3)
    summed = lax.all_to_all(summed, "shot", split_axis=2, concat_axis=3, tiled=True)
    summed = lax.all_gather(summed, "freq", axis=0, tiled=True).reshape(2 * NF, shot_dev, receivers)

    wide = start - HALF + jnp.arange(time_dev + 2 * HALF, dtype=jnp.int32)
    synthesis = basis_rows(wide).astype(BF16).astype(F32).reshape(2 * NF, time_dev + 2 * HALF)
    synthesis = jnp.where((wide >= 0) & (wide < NT), synthesis, 0.0)
    filtered = jnp.zeros((shot_dev, 2 * NF, time_dev), F32)
    for j in range(TAPS):
        tap = filters[:, j].astype(F32)[:, None, None]
        filtered = filtered + tap * synthesis[:, 2 * HALF - j : 2 * HALF - j + time_dev]
    out = jnp.einsum("fsr,sft->srt", summed, filtered.astype(BF16), preferred_element_type=F32)
    return out.astype(BF16)


def solution(mesh):
    in_specs = (
        P("shot", None, "freq"),
        P(),
        P(None, "shot", None),
        P(None, "shot"),
        P("shot", None),
    )
    out_specs = P("shot", None, "freq")
    whole_pieces = mesh.shape["shot"] == 16 and mesh.shape["freq"] == 2
    body = shards if whole_pieces else general_shards
    return jax.shard_map(body, mesh=mesh, in_specs=in_specs, out_specs=out_specs, check_vma=False)
```

time: 30.4 us -> 30.2 us (level)
  Pallas kernels: 8.87 us -> 7.88 us
  waiting for transfers between devices: 4.74 us -> 5.65 us
    pallas_call x1, Pallas kernels: 3.44 us -> 2.11 us  [shards(): pl.pallas_call(tables_kernel, in_specs=[in_smem(), in_vmem(), in_vmem(),...]
    all_to_all x1, waiting for transfers between devices: 4.74 us -> 5.65 us  [shards(): lax.all_to_all(messages, DEVICES, split_axis=0, concat_axis=0, tiled=True)]
  transfers between devices with their start and end apart: 1 -> 1, of which waited for: 1 -> 1; matrix products, arithmetic and copies ran while one was open for 0% -> 0% of each run, Pallas kernels for 11% -> 7%
where the time goes in v2:
time: 30.2 us; the launch traced here: 30 us
  blocking collectives  9.1 us (30%)
  Pallas kernels  7.88 us (26%)
  starting transfers between devices  7.32 us (24%)
  waiting for transfers between devices  5.65 us (19%)
    all_to_all x1, blocking collectives, shards(): lax.all_to_all(messages.reshape(devices, NF, LANES), DEVICES, split_axis=...  9.1 us
    all_to_all x1, starting transfers between devices, shards(): lax.all_to_all(messages, DEVICES, split_axis=0, concat_axis=0, tiled=True)  7.32 us
    all_to_all x1, waiting for transfers between devices, shards(): lax.all_to_all(messages, DEVICES, split_axis=0, concat_axis=0, tiled=True)  5.65 us
    pallas_call x1, Pallas kernels, shards(): pl.pallas_call(analysis_kernel, in_specs=[in_hbm(), in_hbm()], out_specs=...  2.96 us
    pallas_call x1, Pallas kernels, shards(): pl.pallas_call(tables_kernel, in_specs=[in_smem(), in_vmem(), in_vmem(),...  2.11 us
    pallas_call x1, Pallas kernels, shards(): pl.pallas_call(synthesis_kernel, in_specs=[in_vmem(), in_vmem()], out_spe...  2.04 us
    pallas_call x1, Pallas kernels, shards(): pl.pallas_call(product_kernel, in_specs=[in_vmem(), in_vmem(), in_vmem()]...  0.77 us
  transfers between devices with their start and end apart: 1, of which 1 were waited for; matrix products, arithmetic and copies ran while one was open for 0% of the time, Pallas kernels for 7%

profile of v2, /device:TPU:0, one launch (start us, length us, event | category | flops | bytes accessed | tf_op | source)
XLA Modules:
  0.0 30.0 jit_solution(16386858993891982889)
XLA Ops:
  0.0 0.0 copy-start.2
  0.0 0.0 copy-start.3
  0.0 0.0 copy-start.1
  0.0 0.0 copy-start
  0.0 3.0 %shard_map.55 = bf16[32,3,4,128]{3,2,1,0:T(4,128)(2,1)} custom-call(s32[8]{0:T(128)} %bins_ref.1, bf16[2,1024,512]{2,1,0:T(8,128)(2,1)} %traces_hbm.1), custom_call_target="tpu_custom_call" | custom-call | flops 33554432 | bytes 2097152 | tf_op jit(solution)/shard_map/pallas_call | solution.py:205
  3.0 7.3 %all-to-all-start = ((bf16[32,3,4,128]{3,2,1,0:T(4,128)(2,1)}), bf16[32,3,4,128]{3,2,1,0:T(4,128)(2,1)S(1)}, u32[]{:S(2)}, u32[]{:S(2)}) async-start(bf16[32,3,4,128]{3,2,1,0:T(4,128)(2,1)} %shard_map.55), calls=%async_computation | async-start | bytes 196608 | tf_op jit(solution)/shard_map/all_to_all | solution.py:223
  10.3 0.0 copy-done.2
  10.3 0.0 copy-done.3
  10.3 0.0 copy-done.1
  10.3 0.0 copy-done
  10.3 2.1 %shard_map.56 = (f32[32,2048]{1,0:T(8,128)S(1)}, bf16[128,2048]{1,0:T(8,128)(2,1)S(1)}, bf16[2,16,512]{2,1,0:T(8,128)(2,1)S(1)}) custom-call(s32[8]{0:T(128)S(1)} %copy-done.2, s32[32,32,64]{2,1,0:T(8,128)S(1)} %bitcast.3, s32[32,64]{1,0:T(8,128)S(1)} %copy-done.1, bf16[2,31]{1,0:T(2,128)(2,1)S(1)} %copy-done.3), custom_call_target="tpu_custom_call" | custom-call | flops 16777216 | bytes 2097152 | tf_op jit(solution)/shard_map/pallas_call | solution.py:226
  12.5 5.7 %all-to-all-done.received_ref = bf16[32,3,4,128]{3,2,1,0:T(4,128)(2,1)S(1)} async-done(((bf16[32,3,4,128]{3,2,1,0:T(4,128)(2,1)}), bf16[32,3,4,128]{3,2,1,0:T(4,128)(2,1)S(1)}, u32[]{:S(2)}, u32[]{:S(2)}) %all-to-all-start) | async-done | bytes 98336 | tf_op jit(solution)/shard_map/all_to_all | solution.py:223
  18.1 0.8 %shard_map.57 = bf16[256,128]{1,0:T(8,128)(2,1)S(1)} custom-call(bf16[32,3,4,128]{3,2,1,0:T(4,128)(2,1)S(1)} %all-to-all-done.received_ref, f32[32,2048]{1,0:T(8,128)S(1)} %get-tuple-element.8.counts_ref, bf16[128,2048]{1,0:T(8,128)(2,1)S(1)} %get-tuple-element.9.spread_ref), custom_call_target="tpu_custom_call" | custom-call | flops 8388608 | bytes 524288 | tf_op jit(solution)/shard_map/pallas_call | solution.py:240
  18.9 9.1 %all_to_all.10 = bf16[32,8,128]{2,1,0:T(8,128)(2,1)S(1)} all-to-all(bf16[32,8,128]{2,1,0:T(8,128)(2,1)S(1)} %bitcast.5), channel_id=1, replica_groups=mesh['shot'=16,'freq'=2] {'shot','freq'}, dimensions={0} | all-to-all | bytes 131072 | tf_op jit(solution)/shard_map/all_to_all | solution.py:253
  28.0 2.0 %shard_map.58 = bf16[2,1024,512]{2,1,0:T(8,128)(2,1)} custom-call(bf16[256,128]{1,0:T(8,128)(2,1)S(1)} %bitcast.4, bf16[2,16,512]{2,1,0:T(8,128)(2,1)S(1)} %get-tuple-element.10.filtered_ref), custom_call_target="tpu_custom_call" | custom-call | flops 33554432 | bytes 2097152 | tf_op jit(solution)/shard_map/pallas_call | solution.py:257
Async XLA Ops:
  0.0 10.3 %copy-start.2 = (s32[8]{0:T(128)S(1)}, s32[8]{0:T(128)}, u32[]{:S(2)}) copy-start(s32[8]{0:T(128)} %bins_ref.1) | copy-start | bytes 100
  0.0 10.3 %copy-start.3 = (bf16[2,31]{1,0:T(2,128)(2,1)S(1)}, bf16[2,31]{1,0:T(2,128)(2,1)}, u32[]{:S(2)}) copy-start(bf16[2,31]{1,0:T(2,128)(2,1)} %filters_ref.1) | copy-start | bytes 376
  0.0 10.3 %copy-start.1 = (s32[32,64]{1,0:T(8,128)S(1)}, s32[32,64]{1,0:T(8,128)}, u32[]{:S(2)}) copy-start(s32[32,64]{1,0:T(8,128)} %lengths_ref.1) | copy-start | bytes 24580
  0.0 10.3 %copy-start = (s32[32,64,32]{1,2,0:T(8,128)S(1)}, s32[32,64,32]{1,2,0:T(8,128)}, u32[]{:S(2)}) copy-start(s32[32,64,32]{1,2,0:T(8,128)} %param.7) | copy-start | bytes 786436
  3.0 15.1 %all-to-all-start = ((bf16[32,3,4,128]{3,2,1,0:T(4,128)(2,1)}), bf16[32,3,4,128]{3,2,1,0:T(4,128)(2,1)S(1)}, u32[]{:S(2)}, u32[]{:S(2)}) async-start(bf16[32,3,4,128]{3,2,1,0:T(4,128)(2,1)} %shard_map.55), calls=%async_computation | async-start | bytes 196608 | tf_op jit(solution)/shard_map/all_to_all | solution.py:223

commit v3 on v2

--- a/solution.py
+++ b/solution.py
@@ -44,13 +44,13 @@
 
 def analysis_kernel(bins_hbm, traces_hbm, message_ref, bins_ref, traces_ref, basis_ref, traces_sem, bins_sem):
     shot_dev, receivers, time_dev = traces_ref.shape
-    steps = traces_sem.shape[0]
-    block = receivers // steps
+    starts = [0, 3 * LANES, receivers]
+    blocks = list(zip(starts, starts[1:]))
     bins_copy = pltpu.make_async_copy(bins_hbm, bins_ref, bins_sem)
     bins_copy.start()
     copies = []
-    for i in range(steps):
-        rows = pl.ds(i * block, block)
+    for i, (start, end) in enumerate(blocks):
+        rows = pl.ds(start, end - start)
         copy = pltpu.make_async_copy(traces_hbm.at[:, rows, :], traces_ref.at[:, rows, :], traces_sem.at[i])
         copy.start()
         copies.append(copy)
@@ -63,19 +63,19 @@
     low = lane < LANES // 2
     is_station = lane % PIECE == 0
     stations = jnp.zeros((2 * NF, LANES), F32)
-    for i in range(steps):
-        copies[i].wait()
+    for copy, (start, end) in zip(copies, blocks):
+        copy.wait()
         terms = [
             lax.dot_general(
                 basis_ref[...],
-                traces_ref[s, i * block : (i + 1) * block, :],
+                traces_ref[s, start:end, :],
                 (((1,), (1,)), ((), ())),
                 preferred_element_type=F32,
             )
             for s in range(shot_dev)
         ]
-        for j in range(block // LANES):
-            tile = i * (block // LANES) + j
+        for j in range((end - start) // LANES):
+            tile = start // LANES + j
             first, second = [x[:, j * LANES : (j + 1) * LANES] for x in terms]
             for s, x in enumerate((first, second)):
                 marked = jnp.where(is_station, x, 0.0)
@@ -94,9 +94,42 @@
             message_ref[2 * g + h, 2] = slab
 
 
-def tables_kernel(bins_ref, aperture_ref, lengths_ref, filters_ref, counts_ref, spread_ref, filtered_ref, codes_ref):
+def tables_kernel(
+    bins_hbm, filters_hbm, lengths_hbm, aperture_hbm, counts_ref, spread_ref, filtered_ref,
+    bins_ref, filters_ref, lengths_ref, aperture_ref, codes_ref, sems,
+):
+    sources = (bins_hbm, filters_hbm, lengths_hbm, aperture_hbm)
+    targets = (bins_ref, filters_ref, lengths_ref, aperture_ref)
+    copies = [pltpu.make_async_copy(x, y, sems.at[i]) for i, (x, y) in enumerate(zip(sources, targets))]
+    for copy in copies:
+        copy.start()
     shots = aperture_ref.shape[0]
     tiles = counts_ref.shape[1] // LANES
+    lane = lax.broadcasted_iota(jnp.int32, (LANES, LANES), 0)
+    station = lane % PIECE * 4 + lane // PIECE - lax.broadcasted_iota(jnp.int32, (LANES, LANES), 1) // (LANES // 2)
+    for tile in range(tiles):
+        here = jnp.where(station == 2 * tile, 1.0, 0.0)
+        spread_ref[:, tile * LANES : (tile + 1) * LANES] = here.astype(BF16)
+
+    copies[0].wait()
+    copies[1].wait()
+    shot_dev, _, time_dev = filtered_ref.shape
+    width = time_dev + LANES
+    basis, times = basis_in_kernel(bins_ref, lax.axis_index("freq") * time_dev - HALF, width)
+    basis = jnp.where((times >= 0) & (times < NT), basis.astype(BF16).astype(F32), 0.0)
+    taps = filters_ref[...].astype(F32)
+    total = [jnp.zeros((2 * NF, time_dev), F32) for _ in range(shot_dev)]
+    for j in range(TAPS):
+        shift = 2 * HALF - j
+        moved = basis if shift == 0 else pltpu.roll(basis, width - shift, 1)
+        moved = moved[:, :time_dev]
+        for s in range(shot_dev):
+            total[s] = total[s] + taps[s : s + 1, j : j + 1] * moved
+    for s in range(shot_dev):
+        filtered_ref[s] = total[s].astype(BF16)
+
+    copies[2].wait()
+    copies[3].wait()
     for s in range(shots):
         lists = aperture_ref[s]
         codes_ref[pl.ds(s, KMAX, stride=shots), :] = jnp.concatenate([lists, lists], axis=1)
@@ -112,27 +145,6 @@
     for tile in range(tiles):
         counts_ref[:, tile * LANES : (tile + 1) * LANES] = totals[tile].astype(F32)
 
-    lane = lax.broadcasted_iota(jnp.int32, (LANES, LANES), 0)
-    station = lane % PIECE * 4 + lane // PIECE - lax.broadcasted_iota(jnp.int32, (LANES, LANES), 1) // (LANES // 2)
-    for tile in range(tiles):
-        here = jnp.where(station == 2 * tile, 1.0, 0.0)
-        spread_ref[:, tile * LANES : (tile + 1) * LANES] = here.astype(BF16)
-
-    shot_dev, _, time_dev = filtered_ref.shape
-    width = time_dev + LANES
-    basis, times = basis_in_kernel(bins_ref, lax.axis_index("freq") * time_dev - HALF, width)
-    basis = jnp.where((times >= 0) & (times < NT), basis.astype(BF16).astype(F32), 0.0)
-    taps = filters_ref[...].astype(F32)
-    total = [jnp.zeros((2 * NF, time_dev), F32) for _ in range(shot_dev)]
-    for j in range(TAPS):
-        shift = 2 * HALF - j
-        moved = basis if shift == 0 else pltpu.roll(basis, width - shift, 1)
-        moved = moved[:, :time_dev]
-        for s in range(shot_dev):
-            total[s] = total[s] + taps[s : s + 1, j : j + 1] * moved
-    for s in range(shot_dev):
-        filtered_ref[s] = total[s].astype(BF16)
-
 
 def product_kernel(received_ref, counts_ref, spread_ref, message_ref, station_ref, first_ref, second_ref):
     groups = received_ref.shape[0] // 2
@@ -173,8 +185,8 @@
         )
         rows = pl.ds(tile * LANES, LANES)
         for s in range(2):
-            out_ref[s, rows, :] = jnp.dot(
-                spectra[s].T.astype(BF16), filtered_ref[s], preferred_element_type=F32
+            out_ref[s, rows, :] = lax.dot_general(
+                spectra[s].astype(BF16), filtered_ref[s], (((0,), (0,)), ((), ())), preferred_element_type=F32
             ).astype(BF16)
             copy = pltpu.make_async_copy(out_ref.at[s, rows, :], out_hbm.at[s, rows, :], out_sem.at[2 * tile + s])
             copy.start()
@@ -191,17 +203,12 @@
     return pl.BlockSpec(memory_space=pltpu.HBM)
 
 
-def in_smem():
-    return pl.BlockSpec(memory_space=pltpu.SMEM)
-
-
 def shards(traces, frequency_bins, aperture, lengths, filters):
     shot_dev, receivers, time_dev = traces.shape
     devices = lax.axis_size("shot") * lax.axis_size("freq")
     shots = aperture.shape[0]
     params = pltpu.CompilerParams(vmem_limit_bytes=VMEM_LIMIT)
 
-    steps = 2
     messages = pl.pallas_call(
         analysis_kernel,
         in_specs=[in_hbm(), in_hbm()],
@@ -211,7 +218,7 @@
             pltpu.SMEM((NF,), jnp.int32),
             pltpu.VMEM(traces.shape, BF16),
             pltpu.VMEM((2 * NF, time_dev), BF16),
-            pltpu.SemaphoreType.DMA((steps,)),
+            pltpu.SemaphoreType.DMA((2,)),
             pltpu.SemaphoreType.DMA,
         ],
         compiler_params=params,
@@ -223,19 +230,27 @@
     received = lax.all_to_all(messages, DEVICES, split_axis=0, concat_axis=0, tiled=True)
 
     pairs = shots * aperture.shape[1]
+    lists = aperture.transpose(0, 2, 1)
     counts, spread, filtered = pl.pallas_call(
         tables_kernel,
-        in_specs=[in_smem(), in_vmem(), in_vmem(), in_vmem()],
-        out_specs=[in_vmem(), in_vmem(), in_vmem()],
+        in_specs=[in_hbm()] * 4,
+        out_specs=[in_vmem()] * 3,
         out_shape=[
             jax.ShapeDtypeStruct((shots, pairs), F32),
             jax.ShapeDtypeStruct((LANES, pairs), BF16),
             jax.ShapeDtypeStruct((shot_dev, 2 * NF, time_dev), BF16),
         ],
-        scratch_shapes=[pltpu.VMEM((KMAX * shots, LANES), jnp.int32)],
+        scratch_shapes=[
+            pltpu.SMEM((NF,), jnp.int32),
+            pltpu.VMEM(filters.shape, BF16),
+            pltpu.VMEM(lengths.shape, jnp.int32),
+            pltpu.VMEM(lists.shape, jnp.int32),
+            pltpu.VMEM((KMAX * shots, LANES), jnp.int32),
+            pltpu.SemaphoreType.DMA((4,)),
+        ],
         compiler_params=params,
         cost_estimate=pl.CostEstimate(flops=1 << 24, bytes_accessed=1 << 21, transcendentals=0),
-    )(frequency_bins, aperture.transpose(0, 2, 1), lengths, filters)
+    )(*[pltpu.with_memory_space_constraint(x, pltpu.HBM) for x in (frequency_bins, filters, lengths, lists)])
 
     messages = pl.pallas_call(
         product_kernel,

time: 30.2 us -> 29.8 us (0.987)
  Pallas kernels: 7.88 us -> 7.49 us
where the time goes in v3:
time: 29.8 us; the launch traced here: 29.6 us
  blocking collectives  9.1 us (31%)
  Pallas kernels  7.49 us (25%)
  starting transfers between devices  7.3 us (24%)
  waiting for transfers between devices  5.65 us (19%)
    all_to_all x1, blocking collectives, shards(): lax.all_to_all(messages.reshape(devices, NF, LANES), DEVICES, split_axis=...  9.1 us
    all_to_all x1, starting transfers between devices, shards(): lax.all_to_all(messages, DEVICES, split_axis=0, concat_axis=0, tiled=True)  7.3 us
    all_to_all x1, waiting for transfers between devices, shards(): lax.all_to_all(messages, DEVICES, split_axis=0, concat_axis=0, tiled=True)  5.65 us
    pallas_call x1, Pallas kernels, shards(): pl.pallas_call(analysis_kernel, in_specs=[in_hbm(), in_hbm()], out_specs=...  2.83 us
    pallas_call x1, Pallas kernels, shards(): pl.pallas_call(tables_kernel, in_specs=[in_hbm()] * 4, out_specs=[in_vmem...  2.15 us
    pallas_call x1, Pallas kernels, shards(): pl.pallas_call(synthesis_kernel, in_specs=[in_vmem(), in_vmem()], out_spe...  1.74 us
    pallas_call x1, Pallas kernels, shards(): pl.pallas_call(product_kernel, in_specs=[in_vmem(), in_vmem(), in_vmem()]...  0.77 us
  transfers between devices with their start and end apart: 1, of which 1 were waited for; matrix products, arithmetic and copies ran while one was open for 0% of the time, Pallas kernels for 7%

profile of v3, /device:TPU:0, one launch (start us, length us, event | category | flops | bytes accessed | tf_op | source)
XLA Modules:
  0.0 29.6 jit_solution(14110369068822130512)
XLA Ops:
  0.0 2.8 %shard_map.55 = bf16[32,3,4,128]{3,2,1,0:T(4,128)(2,1)} custom-call(s32[8]{0:T(128)} %bins_hbm.3, bf16[2,1024,512]{2,1,0:T(8,128)(2,1)} %traces_hbm.1), custom_call_target="tpu_custom_call" | custom-call | flops 33554432 | bytes 2097152 | tf_op jit(solution)/shard_map/pallas_call | solution.py:212
  2.8 7.3 %all-to-all-start = ((bf16[32,3,4,128]{3,2,1,0:T(4,128)(2,1)}), bf16[32,3,4,128]{3,2,1,0:T(4,128)(2,1)S(1)}, u32[]{:S(2)}, u32[]{:S(2)}) async-start(bf16[32,3,4,128]{3,2,1,0:T(4,128)(2,1)} %shard_map.55), calls=%async_computation | async-start | bytes 196608 | tf_op jit(solution)/shard_map/all_to_all | solution.py:230
  10.1 2.2 %shard_map.56 = (f32[32,2048]{1,0:T(8,128)S(1)}, bf16[128,2048]{1,0:T(8,128)(2,1)S(1)}, bf16[2,16,512]{2,1,0:T(8,128)(2,1)S(1)}) custom-call(s32[8]{0:T(128)} %bins_hbm.3, bf16[2,31]{1,0:T(2,128)(2,1)} %filters_hbm.1, s32[32,64]{1,0:T(8,128)} %lengths_hbm.1, s32[32,32,64]{2,1,0:T(8,128)} %bitcast.5), custom_call_target="tpu_custom_call" | custom-call | flops 16777216 | bytes 2097152 | tf_op jit(solution)/shard_map/pallas_call | solution.py:234
  12.3 5.7 %all-to-all-done.received_ref = bf16[32,3,4,128]{3,2,1,0:T(4,128)(2,1)S(1)} async-done(((bf16[32,3,4,128]{3,2,1,0:T(4,128)(2,1)}), bf16[32,3,4,128]{3,2,1,0:T(4,128)(2,1)S(1)}, u32[]{:S(2)}, u32[]{:S(2)}) %all-to-all-start) | async-done | bytes 98336 | tf_op jit(solution)/shard_map/all_to_all | solution.py:230
  18.0 0.8 %shard_map.57 = bf16[256,128]{1,0:T(8,128)(2,1)S(1)} custom-call(bf16[32,3,4,128]{3,2,1,0:T(4,128)(2,1)S(1)} %all-to-all-done.received_ref, f32[32,2048]{1,0:T(8,128)S(1)} %get-tuple-element.8.counts_ref, bf16[128,2048]{1,0:T(8,128)(2,1)S(1)} %get-tuple-element.9.spread_ref), custom_call_target="tpu_custom_call" | custom-call | flops 8388608 | bytes 524288 | tf_op jit(solution)/shard_map/pallas_call | solution.py:255
  18.7 9.1 %all_to_all.10 = bf16[32,8,128]{2,1,0:T(8,128)(2,1)S(1)} all-to-all(bf16[32,8,128]{2,1,0:T(8,128)(2,1)S(1)} %bitcast.4), channel_id=1, replica_groups=mesh['shot'=16,'freq'=2] {'shot','freq'}, dimensions={0} | all-to-all | bytes 131072 | tf_op jit(solution)/shard_map/all_to_all | solution.py:268
  27.8 1.7 %shard_map.58 = bf16[2,1024,512]{2,1,0:T(8,128)(2,1)} custom-call(bf16[256,128]{1,0:T(8,128)(2,1)S(1)} %bitcast.3, bf16[2,16,512]{2,1,0:T(8,128)(2,1)S(1)} %get-tuple-element.10.filtered_ref), custom_call_target="tpu_custom_call" | custom-call | flops 33554432 | bytes 2097152 | tf_op jit(solution)/shard_map/pallas_call | solution.py:272
Async XLA Ops:
  2.8 15.1 %all-to-all-start = ((bf16[32,3,4,128]{3,2,1,0:T(4,128)(2,1)}), bf16[32,3,4,128]{3,2,1,0:T(4,128)(2,1)S(1)}, u32[]{:S(2)}, u32[]{:S(2)}) async-start(bf16[32,3,4,128]{3,2,1,0:T(4,128)(2,1)} %shard_map.55), calls=%async_computation | async-start | bytes 196608 | tf_op jit(solution)/shard_map/all_to_all | solution.py:230

commit v4 on v3

--- a/solution.py
+++ b/solution.py
@@ -42,21 +42,120 @@
     return cosine((bins * times + part * (NT // 4)) & (NT - 1)), times
 
 
-def analysis_kernel(bins_hbm, traces_hbm, message_ref, bins_ref, traces_ref, basis_ref, traces_sem, bins_sem):
+def write_spread(spread_ref):
+    lane = lax.broadcasted_iota(jnp.int32, (LANES, LANES), 0)
+    station = lane % PIECE * 4 + lane // PIECE - lax.broadcasted_iota(jnp.int32, (LANES, LANES), 1) // (LANES // 2)
+    for tile in range(spread_ref.shape[1] // LANES):
+        here = jnp.where(station == 2 * tile, 1.0, 0.0)
+        spread_ref[:, tile * LANES : (tile + 1) * LANES] = here.astype(BF16)
+
+
+def write_filtered(bins_ref, filters_ref, filtered_ref):
+    shot_dev, _, time_dev = filtered_ref.shape
+    width = time_dev + LANES
+    basis, times = basis_in_kernel(bins_ref, lax.axis_index("freq") * time_dev - HALF, width)
+    basis = jnp.where((times >= 0) & (times < NT), basis.astype(BF16).astype(F32), 0.0)
+    taps = filters_ref[...].astype(F32)
+    total = [jnp.zeros((2 * NF, time_dev), F32) for _ in range(shot_dev)]
+    for j in range(TAPS):
+        shift = 2 * HALF - j
+        moved = basis if shift == 0 else pltpu.roll(basis, width - shift, 1)
+        moved = moved[:, :time_dev]
+        for s in range(shot_dev):
+            total[s] = total[s] + taps[s : s + 1, j : j + 1] * moved
+    for s in range(shot_dev):
+        filtered_ref[s] = total[s].astype(BF16)
+
+
+def bit_sums(words):
+    waiting, planes = [], []
+    for word in words:
+        level = 0
+        while True:
+            if level == len(waiting):
+                waiting.append([])
+            waiting[level].append(word)
+            if len(waiting[level]) < 3:
+                break
+            x, y, z = waiting[level]
+            either = x ^ y
+            waiting[level] = [either ^ z]
+            word = (x & y) | (either & z)
+            level += 1
+    level = 0
+    while level < len(waiting):
+        held = waiting[level]
+        if len(held) > 1:
+            if level + 1 == len(waiting):
+                waiting.append([])
+            x, y = held[0], held[1]
+            carries = [x & y]
+            if len(held) == 3:
+                carries = [(x & y) | ((x ^ y) & held[2])]
+            waiting[level + 1] += carries
+            held = [x ^ y] if len(held) == 2 else [x ^ y ^ held[2]]
+        planes.append(held[0])
+        level += 1
+    return planes
+
+
+def write_counts(aperture_ref, lengths_ref, codes_ref, counts_ref):
+    half = aperture_ref.shape[0] // 2
+    for s in range(half):
+        both = jnp.concatenate([aperture_ref[s], aperture_ref[s + half]], axis=1)
+        codes_ref[pl.ds(s, KMAX, stride=half), :] = both
+    lengths = jnp.concatenate([lengths_ref[:half, :], lengths_ref[half:, :]], axis=1)
+    one = jnp.ones((half, LANES), jnp.int32)
+
+    def words():
+        for k in range(KMAX):
+            codes = codes_ref[k * half : (k + 1) * half, :]
+            yield jnp.where(lengths > k, lax.shift_left(one, codes), 0)
+
+    planes = bit_sums(words())
+    low = lax.broadcasted_iota(jnp.int32, (half, LANES), 1) < LANES // 2
+    for i in range(0, 8, 2):
+        packed = []
+        for bit in (i, i + 1):
+            total = 0
+            for level, plane in enumerate(planes):
+                spread = lax.shift_right_logical(plane, jnp.full_like(plane, bit)) & 0x01010101
+                total = total + (spread << level)
+            packed.append(total)
+        for byte in range(4):
+            left, right = [(lax.shift_right_logical(x, jnp.full_like(x, 8 * byte)) & 255).astype(F32) for x in packed]
+            lanes = pl.ds((8 * byte + i) * (LANES // 2), LANES)
+            counts_ref[:half, lanes] = jnp.where(low, left, pltpu.roll(right, LANES // 2, 1))
+            counts_ref[half:, lanes] = jnp.where(low, pltpu.roll(left, LANES // 2, 1), right)
+
+
+def analysis_kernel(
+    bins_hbm, filters_hbm, lengths_hbm, aperture_hbm, traces_hbm,
+    message_ref, counts_ref, spread_ref, filtered_ref,
+    bins_ref, filters_ref, lengths_ref, aperture_ref, traces_ref, basis_ref, codes_ref, sems,
+):
     shot_dev, receivers, time_dev = traces_ref.shape
+    sources = (bins_hbm, filters_hbm, lengths_hbm, aperture_hbm)
+    targets = (bins_ref, filters_ref, lengths_ref, aperture_ref)
+    tables = [pltpu.make_async_copy(x, y, sems.at[i]) for i, (x, y) in enumerate(zip(sources, targets))]
     starts = [0, 3 * LANES, receivers]
     blocks = list(zip(starts, starts[1:]))
-    bins_copy = pltpu.make_async_copy(bins_hbm, bins_ref, bins_sem)
-    bins_copy.start()
     copies = []
     for i, (start, end) in enumerate(blocks):
         rows = pl.ds(start, end - start)
-        copy = pltpu.make_async_copy(traces_hbm.at[:, rows, :], traces_ref.at[:, rows, :], traces_sem.at[i])
+        copies.append(pltpu.make_async_copy(traces_hbm.at[:, rows, :], traces_ref.at[:, rows, :], sems.at[4 + i]))
+    for copy in tables + copies:
         copy.start()
-        copies.append(copy)
-    bins_copy.wait()
+
+    write_spread(spread_ref)
+    tables[0].wait()
+    tables[1].wait()
     basis, _ = basis_in_kernel(bins_ref, lax.axis_index("freq") * time_dev, time_dev)
     basis_ref[...] = (basis * NT ** (-0.5)).astype(BF16)
+    write_filtered(bins_ref, filters_ref, filtered_ref)
+    tables[2].wait()
+    tables[3].wait()
+    write_counts(aperture_ref, lengths_ref, codes_ref, counts_ref)
 
     lane = lax.broadcasted_iota(jnp.int32, (2 * NF, LANES), 1)
     row = lax.broadcasted_iota(jnp.int32, (2 * NF, LANES), 0)
@@ -94,58 +193,6 @@
             message_ref[2 * g + h, 2] = slab
 
 
-def tables_kernel(
-    bins_hbm, filters_hbm, lengths_hbm, aperture_hbm, counts_ref, spread_ref, filtered_ref,
-    bins_ref, filters_ref, lengths_ref, aperture_ref, codes_ref, sems,
-):
-    sources = (bins_hbm, filters_hbm, lengths_hbm, aperture_hbm)
-    targets = (bins_ref, filters_ref, lengths_ref, aperture_ref)
-    copies = [pltpu.make_async_copy(x, y, sems.at[i]) for i, (x, y) in enumerate(zip(sources, targets))]
-    for copy in copies:
-        copy.start()
-    shots = aperture_ref.shape[0]
-    tiles = counts_ref.shape[1] // LANES
-    lane = lax.broadcasted_iota(jnp.int32, (LANES, LANES), 0)
-    station = lane % PIECE * 4 + lane // PIECE - lax.broadcasted_iota(jnp.int32, (LANES, LANES), 1) // (LANES // 2)
-    for tile in range(tiles):
-        here = jnp.where(station == 2 * tile, 1.0, 0.0)
-        spread_ref[:, tile * LANES : (tile + 1) * LANES] = here.astype(BF16)
-
-    copies[0].wait()
-    copies[1].wait()
-    shot_dev, _, time_dev = filtered_ref.shape
-    width = time_dev + LANES
-    basis, times = basis_in_kernel(bins_ref, lax.axis_index("freq") * time_dev - HALF, width)
-    basis = jnp.where((times >= 0) & (times < NT), basis.astype(BF16).astype(F32), 0.0)
-    taps = filters_ref[...].astype(F32)
-    total = [jnp.zeros((2 * NF, time_dev), F32) for _ in range(shot_dev)]
-    for j in range(TAPS):
-        shift = 2 * HALF - j
-        moved = basis if shift == 0 else pltpu.roll(basis, width - shift, 1)
-        moved = moved[:, :time_dev]
-        for s in range(shot_dev):
-            total[s] = total[s] + taps[s : s + 1, j : j + 1] * moved
-    for s in range(shot_dev):
-        filtered_ref[s] = total[s].astype(BF16)
-
-    copies[2].wait()
-    copies[3].wait()
-    for s in range(shots):
-        lists = aperture_ref[s]
-        codes_ref[pl.ds(s, KMAX, stride=shots), :] = jnp.concatenate([lists, lists], axis=1)
-    lengths = jnp.concatenate([lengths_ref[...]] * 2, axis=1)
-    upper = lax.broadcasted_iota(jnp.int32, (shots, LANES), 1) // (LANES // 2)
-    totals = [jnp.zeros((shots, LANES), BF16) for _ in range(tiles)]
-    for k in range(KMAX):
-        codes = codes_ref[k * shots : (k + 1) * shots, :]
-        codes = jnp.where(lengths > k, codes - upper, -LANES).astype(F32).astype(BF16)
-        for tile in range(tiles):
-            hit = jnp.where(codes == BF16(2 * tile), BF16(1.0), BF16(0.0))
-            totals[tile] = totals[tile] + hit
-    for tile in range(tiles):
-        counts_ref[:, tile * LANES : (tile + 1) * LANES] = totals[tile].astype(F32)
-
-
 def product_kernel(received_ref, counts_ref, spread_ref, message_ref, station_ref, first_ref, second_ref):
     groups = received_ref.shape[0] // 2
     for g in range(groups):
@@ -209,48 +256,30 @@
     shots = aperture.shape[0]
     params = pltpu.CompilerParams(vmem_limit_bytes=VMEM_LIMIT)
 
-    messages = pl.pallas_call(
-        analysis_kernel,
-        in_specs=[in_hbm(), in_hbm()],
-        out_specs=in_vmem(),
-        out_shape=jax.ShapeDtypeStruct((devices, 3, NF // 2, LANES), BF16),
-        scratch_shapes=[
-            pltpu.SMEM((NF,), jnp.int32),
-            pltpu.VMEM(traces.shape, BF16),
-            pltpu.VMEM((2 * NF, time_dev), BF16),
-            pltpu.SemaphoreType.DMA((2,)),
-            pltpu.SemaphoreType.DMA,
-        ],
-        compiler_params=params,
-        cost_estimate=pl.CostEstimate(flops=2 * 16 * traces.size, bytes_accessed=2 * traces.size, transcendentals=0),
-    )(
-        pltpu.with_memory_space_constraint(frequency_bins, pltpu.HBM),
-        pltpu.with_memory_space_constraint(traces, pltpu.HBM),
-    )
-    received = lax.all_to_all(messages, DEVICES, split_axis=0, concat_axis=0, tiled=True)
-
     pairs = shots * aperture.shape[1]
     lists = aperture.transpose(0, 2, 1)
-    counts, spread, filtered = pl.pallas_call(
-        tables_kernel,
-        in_specs=[in_hbm()] * 4,
-        out_specs=[in_vmem()] * 3,
+    operands = (frequency_bins, filters, lengths, lists, traces)
+    messages, counts, spread, filtered = pl.pallas_call(
+        analysis_kernel,
+        in_specs=[in_hbm()] * len(operands),
+        out_specs=[in_vmem()] * 4,
         out_shape=[
+            jax.ShapeDtypeStruct((devices, 3, NF // 2, LANES), BF16),
             jax.ShapeDtypeStruct((shots, pairs), F32),
             jax.ShapeDtypeStruct((LANES, pairs), BF16),
             jax.ShapeDtypeStruct((shot_dev, 2 * NF, time_dev), BF16),
         ],
         scratch_shapes=[
             pltpu.SMEM((NF,), jnp.int32),
-            pltpu.VMEM(filters.shape, BF16),
-            pltpu.VMEM(lengths.shape, jnp.int32),
-            pltpu.VMEM(lists.shape, jnp.int32),
-            pltpu.VMEM((KMAX * shots, LANES), jnp.int32),
-            pltpu.SemaphoreType.DMA((4,)),
+            *[pltpu.VMEM(x.shape, x.dtype) for x in operands[1:]],
+            pltpu.VMEM((2 * NF, time_dev), BF16),
+            pltpu.VMEM((KMAX * shots // 2, LANES), jnp.int32),
+            pltpu.SemaphoreType.DMA((6,)),
         ],
         compiler_params=params,
-        cost_estimate=pl.CostEstimate(flops=1 << 24, bytes_accessed=1 << 21, transcendentals=0),
-    )(*[pltpu.with_memory_space_constraint(x, pltpu.HBM) for x in (frequency_bins, filters, lengths, lists)])
+        cost_estimate=pl.CostEstimate(flops=2 * 16 * traces.size, bytes_accessed=2 * traces.size, transcendentals=0),
+    )(*[pltpu.with_memory_space_constraint(x, pltpu.HBM) for x in operands])
+    received = lax.all_to_all(messages, DEVICES, split_axis=0, concat_axis=0, tiled=True)
 
     messages = pl.pallas_call(
         product_kernel,

time: 29.8 us -> 29.4 us (0.987)
  blocking collectives: 9.1 us -> 24 us
  starting transfers between devices: 7.3 us -> 0 us
  waiting for transfers between devices: 5.65 us -> 0 us
  Pallas kernels: 7.49 us -> 5.14 us
    all_to_all x0 -> x1, blocking collectives: none -> 14.9 us  [shards(): lax.all_to_all(messages, DEVICES, split_axis=0, concat_axis=0, tiled=True)]
    all_to_all x1 -> x0, starting transfers between devices: 7.3 us -> none  [shards(): lax.all_to_all(messages, DEVICES, split_axis=0, concat_axis=0, tiled=True)]
    all_to_all x1 -> x0, waiting for transfers between devices: 5.65 us -> none  [shards(): lax.all_to_all(messages, DEVICES, split_axis=0, concat_axis=0, tiled=True)]
    pallas_call x2 -> x1, Pallas kernels: 4.98 us -> 2.63 us  [shards(): pl.pallas_call(analysis_kernel, in_specs=[in_hbm()] * len(operands), out_...]
  transfers between devices with their start and end apart: 1 -> 0, of which waited for: 1 -> 0; matrix products, arithmetic and copies ran while one was open for 0% -> 0% of each run, Pallas kernels for 7% -> 0%
where the time goes in v4:
time: 29.4 us; the launch traced here: 29.2 us
  blocking collectives  24 us (82%)
  Pallas kernels  5.14 us (17%)
    all_to_all x1, blocking collectives, shards(): lax.all_to_all(messages, DEVICES, split_axis=0, concat_axis=0, tiled=True)  14.9 us
    all_to_all x1, blocking collectives, shards(): lax.all_to_all(messages.reshape(devices, NF, LANES), DEVICES, split_axis=...  9.1 us
    pallas_call x1, Pallas kernels, shards(): pl.pallas_call(analysis_kernel, in_specs=[in_hbm()] * len(operands), out_...  2.63 us
    pallas_call x1, Pallas kernels, shards(): pl.pallas_call(synthesis_kernel, in_specs=[in_vmem(), in_vmem()], out_spe...  1.76 us
    pallas_call x1, Pallas kernels, shards(): pl.pallas_call(product_kernel, in_specs=[in_vmem(), in_vmem(), in_vmem()]...  0.76 us

profile of v4, /device:TPU:0, one launch (start us, length us, event | category | flops | bytes accessed | tf_op | source)
XLA Modules:
  0.0 29.2 jit_solution(200674848854278505)
XLA Ops:
  0.0 2.6 %shard_map.55 = (bf16[32,3,4,128]{3,2,1,0:T(4,128)(2,1)S(1)}, f32[32,2048]{1,0:T(8,128)S(1)}, bf16[128,2048]{1,0:T(8,128)(2,1)S(1)}, bf16[2,16,512]{2,1,0:T(8,128)(2,1)S(1)}) custom-call(s32[8]{0:T(128)} %bins_hbm.1, bf16[2,31]{1,0:T(2,128)(2,1)} %filters_hbm.1, s32[32,64]{1,0:T(8,128)} %lengths_hbm.1, s32[32,32,64]{2,1,0:T(8,128)} %bitcast.5, ...), custom_call_target="tpu_custom_call" | custom-call | flops 33554432 | bytes 2097152 | tf_op jit(solution)/shard_map/pallas_call | solution.py:262
  2.6 14.9 %all_to_all.10.received_ref = bf16[32,3,4,128]{3,2,1,0:T(4,128)(2,1)S(1)} all-to-all(bf16[32,3,4,128]{3,2,1,0:T(4,128)(2,1)S(1)} %get-tuple-element.9), channel_id=1, replica_groups=mesh['shot'=16,'freq'=2] {'shot','freq'}, dimensions={0} | all-to-all | bytes 196608 | tf_op jit(solution)/shard_map/all_to_all | solution.py:282
  17.6 0.8 %shard_map.56 = bf16[256,128]{1,0:T(8,128)(2,1)S(1)} custom-call(bf16[32,3,4,128]{3,2,1,0:T(4,128)(2,1)S(1)} %all_to_all.10.received_ref, f32[32,2048]{1,0:T(8,128)S(1)} %get-tuple-element.10.counts_ref, bf16[128,2048]{1,0:T(8,128)(2,1)S(1)} %get-tuple-element.11.spread_ref), custom_call_target="tpu_custom_call" | custom-call | flops 8388608 | bytes 524288 | tf_op jit(solution)/shard_map/pallas_call | solution.py:284
  18.3 9.1 %all_to_all.11 = bf16[32,8,128]{2,1,0:T(8,128)(2,1)S(1)} all-to-all(bf16[32,8,128]{2,1,0:T(8,128)(2,1)S(1)} %bitcast.4), channel_id=1, replica_groups=mesh['shot'=16,'freq'=2] {'shot','freq'}, dimensions={0} | all-to-all | bytes 131072 | tf_op jit(solution)/shard_map/all_to_all | solution.py:297
  27.4 1.8 %shard_map.57 = bf16[2,1024,512]{2,1,0:T(8,128)(2,1)} custom-call(bf16[256,128]{1,0:T(8,128)(2,1)S(1)} %bitcast.3, bf16[2,16,512]{2,1,0:T(8,128)(2,1)S(1)} %get-tuple-element.12.filtered_ref), custom_call_target="tpu_custom_call" | custom-call | flops 33554432 | bytes 2097152 | tf_op jit(solution)/shard_map/pallas_call | solution.py:301

commit v5 on v4

--- a/solution.py
+++ b/solution.py
@@ -153,9 +153,6 @@
     basis, _ = basis_in_kernel(bins_ref, lax.axis_index("freq") * time_dev, time_dev)
     basis_ref[...] = (basis * NT ** (-0.5)).astype(BF16)
     write_filtered(bins_ref, filters_ref, filtered_ref)
-    tables[2].wait()
-    tables[3].wait()
-    write_counts(aperture_ref, lengths_ref, codes_ref, counts_ref)
 
     lane = lax.broadcasted_iota(jnp.int32, (2 * NF, LANES), 1)
     row = lax.broadcasted_iota(jnp.int32, (2 * NF, LANES), 0)
@@ -164,6 +161,10 @@
     stations = jnp.zeros((2 * NF, LANES), F32)
     for copy, (start, end) in zip(copies, blocks):
         copy.wait()
+        if end == receivers:
+            tables[2].wait()
+            tables[3].wait()
+            write_counts(aperture_ref, lengths_ref, codes_ref, counts_ref)
         terms = [
             lax.dot_general(
                 basis_ref[...],

time: 29.4 us -> 29.2 us (level)
  no operation moved by 1% of the time
where the time goes in v5:
time: 29.2 us; the launch traced here: 29 us
  blocking collectives  24 us (82%)
  Pallas kernels  4.96 us (17%)
    all_to_all x1, blocking collectives, shards(): lax.all_to_all(messages, DEVICES, split_axis=0, concat_axis=0, tiled=True)  14.9 us
    all_to_all x1, blocking collectives, shards(): lax.all_to_all(messages.reshape(devices, NF, LANES), DEVICES, split_axis=...  9.1 us
    pallas_call x1, Pallas kernels, shards(): pl.pallas_call(analysis_kernel, in_specs=[in_hbm()] * len(operands), out_...  2.45 us
    pallas_call x1, Pallas kernels, shards(): pl.pallas_call(synthesis_kernel, in_specs=[in_vmem(), in_vmem()], out_spe...  1.75 us
    pallas_call x1, Pallas kernels, shards(): pl.pallas_call(product_kernel, in_specs=[in_vmem(), in_vmem(), in_vmem()]...  0.76 us

profile of v5, /device:TPU:0, one launch (start us, length us, event | category | flops | bytes accessed | tf_op | source)
XLA Modules:
  0.0 29.0 jit_solution(11660582494842413207)
XLA Ops:
  0.0 2.5 %shard_map.55 = (bf16[32,3,4,128]{3,2,1,0:T(4,128)(2,1)S(1)}, f32[32,2048]{1,0:T(8,128)S(1)}, bf16[128,2048]{1,0:T(8,128)(2,1)S(1)}, bf16[2,16,512]{2,1,0:T(8,128)(2,1)S(1)}) custom-call(s32[8]{0:T(128)} %bins_hbm.1, bf16[2,31]{1,0:T(2,128)(2,1)} %filters_hbm.1, s32[32,64]{1,0:T(8,128)} %lengths_hbm.1, s32[32,32,64]{2,1,0:T(8,128)} %bitcast.5, ...), custom_call_target="tpu_custom_call" | custom-call | flops 33554432 | bytes 2097152 | tf_op jit(solution)/shard_map/pallas_call | solution.py:263
  2.5 14.9 %all_to_all.10.received_ref = bf16[32,3,4,128]{3,2,1,0:T(4,128)(2,1)S(1)} all-to-all(bf16[32,3,4,128]{3,2,1,0:T(4,128)(2,1)S(1)} %get-tuple-element.9), channel_id=1, replica_groups=mesh['shot'=16,'freq'=2] {'shot','freq'}, dimensions={0} | all-to-all | bytes 196608 | tf_op jit(solution)/shard_map/all_to_all | solution.py:283
  17.4 0.8 %shard_map.56 = bf16[256,128]{1,0:T(8,128)(2,1)S(1)} custom-call(bf16[32,3,4,128]{3,2,1,0:T(4,128)(2,1)S(1)} %all_to_all.10.received_ref, f32[32,2048]{1,0:T(8,128)S(1)} %get-tuple-element.10.counts_ref, bf16[128,2048]{1,0:T(8,128)(2,1)S(1)} %get-tuple-element.11.spread_ref), custom_call_target="tpu_custom_call" | custom-call | flops 8388608 | bytes 524288 | tf_op jit(solution)/shard_map/pallas_call | solution.py:285
  18.1 9.1 %all_to_all.11 = bf16[32,8,128]{2,1,0:T(8,128)(2,1)S(1)} all-to-all(bf16[32,8,128]{2,1,0:T(8,128)(2,1)S(1)} %bitcast.4), channel_id=1, replica_groups=mesh['shot'=16,'freq'=2] {'shot','freq'}, dimensions={0} | all-to-all | bytes 131072 | tf_op jit(solution)/shard_map/all_to_all | solution.py:298
  27.2 1.8 %shard_map.57 = bf16[2,1024,512]{2,1,0:T(8,128)(2,1)} custom-call(bf16[256,128]{1,0:T(8,128)(2,1)S(1)} %bitcast.3, bf16[2,16,512]{2,1,0:T(8,128)(2,1)S(1)} %get-tuple-element.12.filtered_ref), custom_call_target="tpu_custom_call" | custom-call | flops 33554432 | bytes 2097152 | tf_op jit(solution)/shard_map/pallas_call | solution.py:302

commit v6 on v5

--- a/solution.py
+++ b/solution.py
@@ -15,6 +15,15 @@
 LANES = 128
 PIECE = 32
 DEVICES = ("shot", "freq")
+CHIPS = 16
+ORDER = [11] + [g for g in range(CHIPS) if g != 11]
+PLACES = [ORDER.index(g) for g in range(CHIPS)]
+
+
+def core_groups(run):
+    return [[2 * g + (core + g // run) % 2 for g in ORDER] for core in range(2)]
+
+
 F32 = jnp.float32
 BF16 = jnp.bfloat16
 VMEM_LIMIT = 48 * 1024 * 1024
@@ -183,50 +192,57 @@
                 stations = stations + (pltpu.roll(marked, shift, 1) if shift else marked)
             even = jnp.where(low, first, pltpu.roll(second, LANES // 2, 1))
             odd = jnp.where(low, pltpu.roll(first, LANES // 2, 1), second)
-            for g, x in ((2 * tile, even), (2 * tile + 1, odd)):
-                for h in range(2):
-                    message_ref[2 * g + h, 0] = x[8 * h : 8 * h + 4].astype(BF16)
-                    message_ref[2 * g + h, 1] = x[8 * h + 4 : 8 * h + 8].astype(BF16)
+            message_ref[PLACES[2 * tile], : 2 * NF] = even.astype(BF16)
+            message_ref[PLACES[2 * tile + 1], : 2 * NF] = odd.astype(BF16)
     stations = jnp.where(row // 4 % 2 == 1, pltpu.roll(stations, 16, 1), stations)
-    for h in range(2):
-        slab = (stations[8 * h : 8 * h + 4] + stations[8 * h + 4 : 8 * h + 8]).astype(BF16)
-        for g in range(message_ref.shape[0] // 2):
-            message_ref[2 * g + h, 2] = slab
-
-
-def product_kernel(received_ref, counts_ref, spread_ref, message_ref, station_ref, first_ref, second_ref):
-    groups = received_ref.shape[0] // 2
-    for g in range(groups):
-        rounded = (received_ref[2 * g].astype(F32) + received_ref[2 * g + 1].astype(F32)).astype(BF16).astype(F32)
-        second_ref[:, g * LANES : (g + 1) * LANES] = jnp.concatenate([rounded[0], rounded[1]], axis=0)
-        legs = [rounded[2]] + [pltpu.roll(rounded[2], LANES - shift, 1) for shift in (16, 8, 24)]
-        station_ref[16 * g : 16 * g + 16, :] = jnp.concatenate(legs, axis=0).astype(BF16)
-    first_ref[...] = jnp.dot(station_ref[...], spread_ref[...], preferred_element_type=F32)
-    second = second_ref[...]
-    crossed = jnp.concatenate([second[4:], second[:4]], axis=0)
+    slabs = [stations[8 * h : 8 * h + 4] + stations[8 * h + 4 : 8 * h + 8] for h in range(2)]
+    slab = jnp.concatenate(slabs, axis=0).astype(BF16)
+    for g in range(message_ref.shape[0]):
+        message_ref[g, 2 * NF :] = slab
+
+
+def product_kernel(
+    own_ref, other_ref, counts_ref, spread_ref, message_ref, station_ref, first_ref, second_ref
+):
+    groups = own_ref.shape[0]
     upper = lax.broadcasted_iota(jnp.int32, (NF, LANES), 0) >= 4
     low = lax.broadcasted_iota(jnp.int32, (NF, LANES), 1) < LANES // 2
+    for g in range(groups):
+        place = PLACES[g]
+        rounded = (own_ref[place].astype(F32) + other_ref[place].astype(F32)).astype(BF16).astype(F32)
+        second_ref[:, g * LANES : (g + 1) * LANES] = rounded[: 2 * NF]
+        stations = rounded[2 * NF :]
+        for s in range(2):
+            real = stations if s == 0 else pltpu.roll(stations, LANES - 8, 1)
+            imag = pltpu.roll(stations, LANES - 16 - 8 * s, 1)
+            legs = [jnp.where(upper, pltpu.roll(imag, 4, 0), real), jnp.where(upper, imag, pltpu.roll(real, 4, 0))]
+            station_ref[32 * g + 16 * s : 32 * g + 16 * s + 16, :] = jnp.concatenate(legs, axis=0).astype(BF16)
+    first_ref[...] = jnp.dot(station_ref[...], spread_ref[...], preferred_element_type=F32)
 
     def total(x):
         x = sum(x[:, i * LANES : (i + 1) * LANES] for i in range(x.shape[1] // LANES))
         return x + pltpu.roll(x, LANES // 2, 1)
 
+    second = [second_ref[NF * h : NF * (h + 1), :] for h in range(2)]
+    crossed = [jnp.concatenate([x[4:], x[:4]], axis=0) for x in second]
     for g in range(groups):
-        spectra = []
-        for s in (2 * g, 2 * g + 1):
-            first = counts_ref[s : s + 1, :] * first_ref[8 * s : 8 * s + 8, :]
-            same, other = total(first * second), total(first * crossed)
-            same, other = same - pltpu.roll(same, 4, 0), other + pltpu.roll(other, 4, 0)
-            spectra.append(jnp.where(upper, other, same) * KMAX ** (-0.5))
-        message = jnp.where(low, spectra[0], spectra[1])
-        message_ref[16 * g : 16 * g + 16, :] = jnp.concatenate([message, message], axis=0).astype(BF16)
+        message = []
+        for h in range(2):
+            spectra = []
+            for s in (2 * g, 2 * g + 1):
+                first = counts_ref[s : s + 1, :] * first_ref[16 * s + 8 * h : 16 * s + 8 * h + 8, :]
+                same, other = total(first * second[h]), total(first * crossed[h])
+                same, other = same - pltpu.roll(same, 4, 0), other + pltpu.roll(other, 4, 0)
+                spectra.append(jnp.where(upper, other, same) * KMAX ** (-0.5))
+            message.append(jnp.where(low, spectra[0], spectra[1]))
+        message_ref[PLACES[g]] = jnp.concatenate(message, axis=0).astype(BF16)
 
 
 def synthesis_kernel(received_ref, filtered_ref, out_hbm, out_ref, out_sem):
     low = lax.broadcasted_iota(jnp.int32, (2 * NF, LANES), 1) < LANES // 2
     copies = []
     for tile in range(out_ref.shape[1] // LANES):
-        left, right = [received_ref[32 * tile + i : 32 * tile + i + 16, :].astype(F32) for i in (0, 16)]
+        left, right = [received_ref[PLACES[2 * tile + i]].astype(F32) for i in range(2)]
         spectra = (
             jnp.where(low, left, pltpu.roll(right, LANES // 2, 1)),
             jnp.where(low, pltpu.roll(left, LANES // 2, 1), right),
@@ -251,9 +267,14 @@
     return pl.BlockSpec(memory_space=pltpu.HBM)
 
 
+def exchange(messages, run):
+    return lax.all_to_all(
+        messages, DEVICES, split_axis=0, concat_axis=0, tiled=True, axis_index_groups=core_groups(run)
+    )
+
+
 def shards(traces, frequency_bins, aperture, lengths, filters):
     shot_dev, receivers, time_dev = traces.shape
-    devices = lax.axis_size("shot") * lax.axis_size("freq")
     shots = aperture.shape[0]
     params = pltpu.CompilerParams(vmem_limit_bytes=VMEM_LIMIT)
 
@@ -265,7 +286,7 @@
         in_specs=[in_hbm()] * len(operands),
         out_specs=[in_vmem()] * 4,
         out_shape=[
-            jax.ShapeDtypeStruct((devices, 3, NF // 2, LANES), BF16),
+            jax.ShapeDtypeStruct((CHIPS, 3 * NF, LANES), BF16),
             jax.ShapeDtypeStruct((shots, pairs), F32),
             jax.ShapeDtypeStruct((LANES, pairs), BF16),
             jax.ShapeDtypeStruct((shot_dev, 2 * NF, time_dev), BF16),
@@ -280,24 +301,23 @@
         compiler_params=params,
         cost_estimate=pl.CostEstimate(flops=2 * 16 * traces.size, bytes_accessed=2 * traces.size, transcendentals=0),
     )(*[pltpu.with_memory_space_constraint(x, pltpu.HBM) for x in operands])
-    received = lax.all_to_all(messages, DEVICES, split_axis=0, concat_axis=0, tiled=True)
+    own = exchange(messages, 4)
+    other = lax.ppermute(own, "freq", [(0, 1), (1, 0)])
 
     messages = pl.pallas_call(
         product_kernel,
-        in_specs=[in_vmem(), in_vmem(), in_vmem()],
+        in_specs=[in_vmem()] * 4,
         out_specs=in_vmem(),
-        out_shape=jax.ShapeDtypeStruct((devices * NF, LANES), BF16),
+        out_shape=jax.ShapeDtypeStruct((CHIPS, 2 * NF, LANES), BF16),
         scratch_shapes=[
-            pltpu.VMEM((shots * NF, LANES), BF16),
-            pltpu.VMEM((shots * NF, pairs), F32),
-            pltpu.VMEM((NF, pairs), F32),
+            pltpu.VMEM((shots * 2 * NF, LANES), BF16),
+            pltpu.VMEM((shots * 2 * NF, pairs), F32),
+            pltpu.VMEM((2 * NF, pairs), F32),
         ],
         compiler_params=params,
-        cost_estimate=pl.CostEstimate(flops=1 << 23, bytes_accessed=1 << 19, transcendentals=0),
-    )(received, counts, spread)
-    received = lax.all_to_all(
-        messages.reshape(devices, NF, LANES), DEVICES, split_axis=0, concat_axis=0, tiled=True
-    ).reshape(devices * NF, LANES)
+        cost_estimate=pl.CostEstimate(flops=1 << 24, bytes_accessed=1 << 20, transcendentals=0),
+    )(own, other, counts, spread)
+    received = exchange(messages, 8)
 
     return pl.pallas_call(
         synthesis_kernel,

time: 29.2 us -> 28.3 us (0.969)
  blocking collectives: 24 us -> 21.2 us
  waiting for transfers between devices: 0 us -> 1.09 us
  Pallas kernels: 4.96 us -> 5.41 us
    all_to_all x2, blocking collectives: 24 us -> 21.2 us  [exchange(): lax.all_to_all(messages, DEVICES, split_axis=0, concat_axis=0, tiled=True...]
    ppermute x0 -> x1, waiting for transfers between devices: none -> 1.09 us  [shards(): other = lax.ppermute(own, 'freq', [(0, 1), (1, 0)])]
    pallas_call x1, Pallas kernels: 0.76 us -> 1.2 us  [shards(): pl.pallas_call(product_kernel, in_specs=[in_vmem()] * 4, out_specs=in_vme...]
  transfers between devices with their start and end apart: 0 -> 1, of which waited for: 0 -> 1; matrix products, arithmetic and copies ran while one was open for 0% -> 0% of each run, Pallas kernels for 0% -> 0%
where the time goes in v6:
time: 28.3 us; the launch traced here: 27.9 us
  blocking collectives  21.2 us (75%)
  Pallas kernels  5.41 us (19%)
  waiting for transfers between devices  1.09 us (4%)
    all_to_all x2, blocking collectives, exchange(): lax.all_to_all(messages, DEVICES, split_axis=0, concat_axis=0, tiled=True...  21.2 us
    pallas_call x1, Pallas kernels, shards(): pl.pallas_call(analysis_kernel, in_specs=[in_hbm()] * len(operands), out_...  2.45 us
    pallas_call x1, Pallas kernels, shards(): pl.pallas_call(synthesis_kernel, in_specs=[in_vmem(), in_vmem()], out_spe...  1.76 us
    pallas_call x1, Pallas kernels, shards(): pl.pallas_call(product_kernel, in_specs=[in_vmem()] * 4, out_specs=in_vme...  1.2 us
    ppermute x1, waiting for transfers between devices, shards(): other = lax.ppermute(own, 'freq', [(0, 1), (1, 0)])  1.09 us
  transfers between devices with their start and end apart: 1, of which 1 were waited for; matrix products, arithmetic and copies ran while one was open for 0% of the time, Pallas kernels for 0%

profile of v6, /device:TPU:0, one launch (start us, length us, event | category | flops | bytes accessed | tf_op | source)
XLA Modules:
  0.0 27.9 jit_solution(6635804948794209761)
XLA Ops:
  0.0 2.5 %shard_map.55 = (bf16[16,24,128]{2,1,0:T(8,128)(2,1)S(1)}, f32[32,2048]{1,0:T(8,128)S(1)}, bf16[128,2048]{1,0:T(8,128)(2,1)S(1)}, bf16[2,16,512]{2,1,0:T(8,128)(2,1)S(1)}) custom-call(s32[8]{0:T(128)} %bins_hbm.1, bf16[2,31]{1,0:T(2,128)(2,1)} %filters_hbm.1, s32[32,64]{1,0:T(8,128)} %lengths_hbm.1, s32[32,32,64]{2,1,0:T(8,128)} %bitcast.1, ...), custom_call_target="tpu_custom_call" | custom-call | flops 33554432 | bytes 2097152 | tf_op jit(solution)/shard_map/pallas_call | solution.py:284
  2.5 12.2 %all_to_all.10.own_ref = bf16[16,24,128]{2,1,0:T(8,128)(2,1)S(1)} all-to-all(bf16[16,24,128]{2,1,0:T(8,128)(2,1)S(1)} %get-tuple-element.9), channel_id=1, replica_groups={{22,0,2,4,6,9,11,13,15,16,18,20,25,27,29,31},{23,1,3,5,7,8,10,12,14,17,..., dimensions={0} | all-to-all | bytes 196608 | tf_op jit(solution)/shard_map/all_to_all | solution.py:271
  14.7 0.2 collective-permute-start
  14.9 1.1 %collective-permute-done.other_ref = bf16[16,24,128]{2,1,0:T(8,128)(2,1)S(1)} collective-permute-done((bf16[16,24,128]{2,1,0:T(8,128)(2,1)S(1)}, bf16[16,24,128]{2,1,0:T(8,128)(2,1)S(1)}, u32[]{:S(2)}, u32[]{:S(2)}) %collective-permute-start) | collective-permute-done | bytes 98336 | tf_op jit(solution)/shard_map/ppermute | solution.py:305
  16.0 1.2 %shard_map.56 = bf16[16,16,128]{2,1,0:T(8,128)(2,1)S(1)} custom-call(bf16[16,24,128]{2,1,0:T(8,128)(2,1)S(1)} %all_to_all.10.own_ref, bf16[16,24,128]{2,1,0:T(8,128)(2,1)S(1)} %collective-permute-done.other_ref, f32[32,2048]{1,0:T(8,128)S(1)} %get-tuple-element.10.counts_ref, bf16[128,2048]{1,0:T(8,128)(2,1)S(1)} %get-tuple-element.11.spread_ref), custom_call_target="tpu_custom_call" | custom-call | flops 16777216 | bytes 1048576 | tf_op jit(solution)/shard_map/pallas_call | solution.py:307
  17.2 8.9 %all_to_all.11.received_ref = bf16[16,16,128]{2,1,0:T(8,128)(2,1)S(1)} all-to-all(bf16[16,16,128]{2,1,0:T(8,128)(2,1)S(1)} %shard_map.56), channel_id=1, replica_groups={{23,0,2,4,6,8,10,12,14,17,19,21,25,27,29,31},{22,1,3,5,7,9,11,13,15,16,..., dimensions={0} | all-to-all | bytes 131072 | tf_op jit(solution)/shard_map/all_to_all | solution.py:271
  26.1 1.8 %shard_map.57 = bf16[2,1024,512]{2,1,0:T(8,128)(2,1)} custom-call(bf16[16,16,128]{2,1,0:T(8,128)(2,1)S(1)} %all_to_all.11.received_ref, bf16[2,16,512]{2,1,0:T(8,128)(2,1)S(1)} %get-tuple-element.12.filtered_ref), custom_call_target="tpu_custom_call" | custom-call | flops 33554432 | bytes 2097152 | tf_op jit(solution)/shard_map/pallas_call | solution.py:322
Async XLA Ops:
  14.7 1.3 %collective-permute-start = (bf16[16,24,128]{2,1,0:T(8,128)(2,1)S(1)}, bf16[16,24,128]{2,1,0:T(8,128)(2,1)S(1)}, u32[]{:S(2)}, u32[]{:S(2)}) collective-permute-start(bf16[16,24,128]{2,1,0:T(8,128)(2,1)S(1)} %all_to_all.10.own_ref), channel_id=1, source_target_pairs={{0,1},{1,0},{2,3},{3,2},{4,5},{5,4},{6,7},{7,6},{8,9},{9,8},{10,11... | collective-permute-start | bytes 294920 | tf_op jit(solution)/shard_map/ppermute | solution.py:305

commit v7 on v6

--- a/solution.py
+++ b/solution.py
@@ -59,11 +59,10 @@
         spread_ref[:, tile * LANES : (tile + 1) * LANES] = here.astype(BF16)
 
 
-def write_filtered(bins_ref, filters_ref, filtered_ref):
+def write_filtered(wide_ref, filters_ref, filtered_ref):
     shot_dev, _, time_dev = filtered_ref.shape
-    width = time_dev + LANES
-    basis, times = basis_in_kernel(bins_ref, lax.axis_index("freq") * time_dev - HALF, width)
-    basis = jnp.where((times >= 0) & (times < NT), basis.astype(BF16).astype(F32), 0.0)
+    basis = wide_ref[...].astype(F32)
+    width = basis.shape[1]
     taps = filters_ref[...].astype(F32)
     total = [jnp.zeros((2 * NF, time_dev), F32) for _ in range(shot_dev)]
     for j in range(TAPS):
@@ -138,30 +137,33 @@
             counts_ref[half:, lanes] = jnp.where(low, pltpu.roll(left, LANES // 2, 1), right)
 
 
+def tables_kernel(
+    wide_ref, filters_ref, lengths_ref, aperture_ref, _, counts_ref, filtered_ref, codes_ref
+):
+    write_counts(aperture_ref, lengths_ref, codes_ref, counts_ref)
+    write_filtered(wide_ref, filters_ref, filtered_ref)
+
+
 def analysis_kernel(
-    bins_hbm, filters_hbm, lengths_hbm, aperture_hbm, traces_hbm,
-    message_ref, counts_ref, spread_ref, filtered_ref,
-    bins_ref, filters_ref, lengths_ref, aperture_ref, traces_ref, basis_ref, codes_ref, sems,
+    bins_hbm, traces_hbm, message_ref, spread_ref, wide_ref, bins_ref, traces_ref, basis_ref, sems,
 ):
     shot_dev, receivers, time_dev = traces_ref.shape
-    sources = (bins_hbm, filters_hbm, lengths_hbm, aperture_hbm)
-    targets = (bins_ref, filters_ref, lengths_ref, aperture_ref)
-    tables = [pltpu.make_async_copy(x, y, sems.at[i]) for i, (x, y) in enumerate(zip(sources, targets))]
+    bins_copy = pltpu.make_async_copy(bins_hbm, bins_ref, sems.at[0])
     starts = [0, 3 * LANES, receivers]
     blocks = list(zip(starts, starts[1:]))
     copies = []
     for i, (start, end) in enumerate(blocks):
         rows = pl.ds(start, end - start)
-        copies.append(pltpu.make_async_copy(traces_hbm.at[:, rows, :], traces_ref.at[:, rows, :], sems.at[4 + i]))
-    for copy in tables + copies:
+        copies.append(pltpu.make_async_copy(traces_hbm.at[:, rows, :], traces_ref.at[:, rows, :], sems.at[1 + i]))
+    for copy in [bins_copy] + copies:
         copy.start()
 
     write_spread(spread_ref)
-    tables[0].wait()
-    tables[1].wait()
-    basis, _ = basis_in_kernel(bins_ref, lax.axis_index("freq") * time_dev, time_dev)
+    bins_copy.wait()
+    wide, times = basis_in_kernel(bins_ref, lax.axis_index("freq") * time_dev - HALF, wide_ref.shape[1])
+    wide_ref[...] = jnp.where((times >= 0) & (times < NT), wide, 0.0).astype(BF16)
+    basis = pltpu.roll(wide, wide.shape[1] - HALF, 1)[:, :time_dev]
     basis_ref[...] = (basis * NT ** (-0.5)).astype(BF16)
-    write_filtered(bins_ref, filters_ref, filtered_ref)
 
     lane = lax.broadcasted_iota(jnp.int32, (2 * NF, LANES), 1)
     row = lax.broadcasted_iota(jnp.int32, (2 * NF, LANES), 0)
@@ -170,10 +172,6 @@
     stations = jnp.zeros((2 * NF, LANES), F32)
     for copy, (start, end) in zip(copies, blocks):
         copy.wait()
-        if end == receivers:
-            tables[2].wait()
-            tables[3].wait()
-            write_counts(aperture_ref, lengths_ref, codes_ref, counts_ref)
         terms = [
             lax.dot_general(
                 basis_ref[...],
@@ -202,7 +200,7 @@
 
 
 def product_kernel(
-    own_ref, other_ref, counts_ref, spread_ref, message_ref, station_ref, first_ref, second_ref
+    own_ref, other_ref, counts_ref, spread_ref, message_ref, station_ref, first_ref, second_ref, same_ref, cross_ref
 ):
     groups = own_ref.shape[0]
     upper = lax.broadcasted_iota(jnp.int32, (NF, LANES), 0) >= 4
@@ -219,21 +217,32 @@
             station_ref[32 * g + 16 * s : 32 * g + 16 * s + 16, :] = jnp.concatenate(legs, axis=0).astype(BF16)
     first_ref[...] = jnp.dot(station_ref[...], spread_ref[...], preferred_element_type=F32)
 
-    def total(x):
-        x = sum(x[:, i * LANES : (i + 1) * LANES] for i in range(x.shape[1] // LANES))
-        return x + pltpu.roll(x, LANES // 2, 1)
-
-    second = [second_ref[NF * h : NF * (h + 1), :] for h in range(2)]
-    crossed = [jnp.concatenate([x[4:], x[:4]], axis=0) for x in second]
+    tiles = second_ref.shape[1] // LANES
+    span = 4
+    for start in range(0, tiles, span):
+        columns = [slice(t * LANES, (t + 1) * LANES) for t in range(start, start + span)]
+        second = [[second_ref[NF * h : NF * (h + 1), c] for c in columns] for h in range(2)]
+        crossed = [[jnp.concatenate([x[4:], x[:4]], axis=0) for x in half] for half in second]
+        for s in range(2 * groups):
+            counts = [counts_ref[s : s + 1, c] for c in columns]
+            for h in range(2):
+                rows = slice(16 * s + 8 * h, 16 * s + 8 * h + 8)
+                first = [count * first_ref[rows, c] for count, c in zip(counts, columns)]
+                same = sum(x * y for x, y in zip(first, second[h]))
+                cross = sum(x * y for x, y in zip(first, crossed[h]))
+                if start:
+                    same, cross = same + same_ref[rows, :], cross + cross_ref[rows, :]
+                same_ref[rows, :] = same
+                cross_ref[rows, :] = cross
     for g in range(groups):
         message = []
         for h in range(2):
             spectra = []
             for s in (2 * g, 2 * g + 1):
-                first = counts_ref[s : s + 1, :] * first_ref[16 * s + 8 * h : 16 * s + 8 * h + 8, :]
-                same, other = total(first * second[h]), total(first * crossed[h])
-                same, other = same - pltpu.roll(same, 4, 0), other + pltpu.roll(other, 4, 0)
-                spectra.append(jnp.where(upper, other, same) * KMAX ** (-0.5))
+                rows = slice(16 * s + 8 * h, 16 * s + 8 * h + 8)
+                same, cross = same_ref[rows, :], cross_ref[rows, :]
+                total = jnp.where(upper, cross + pltpu.roll(cross, 4, 0), same - pltpu.roll(same, 4, 0))
+                spectra.append((total + pltpu.roll(total, LANES // 2, 1)) * KMAX ** (-0.5))
             message.append(jnp.where(low, spectra[0], spectra[1]))
         message_ref[PLACES[g]] = jnp.concatenate(message, axis=0).astype(BF16)
 
@@ -279,30 +288,39 @@
     params = pltpu.CompilerParams(vmem_limit_bytes=VMEM_LIMIT)
 
     pairs = shots * aperture.shape[1]
-    lists = aperture.transpose(0, 2, 1)
-    operands = (frequency_bins, filters, lengths, lists, traces)
-    messages, counts, spread, filtered = pl.pallas_call(
+    operands = (frequency_bins, traces)
+    messages, spread, wide = pl.pallas_call(
         analysis_kernel,
         in_specs=[in_hbm()] * len(operands),
-        out_specs=[in_vmem()] * 4,
+        out_specs=[in_vmem()] * 3,
         out_shape=[
             jax.ShapeDtypeStruct((CHIPS, 3 * NF, LANES), BF16),
-            jax.ShapeDtypeStruct((shots, pairs), F32),
             jax.ShapeDtypeStruct((LANES, pairs), BF16),
-            jax.ShapeDtypeStruct((shot_dev, 2 * NF, time_dev), BF16),
+            jax.ShapeDtypeStruct((2 * NF, time_dev + LANES), BF16),
         ],
         scratch_shapes=[
             pltpu.SMEM((NF,), jnp.int32),
             *[pltpu.VMEM(x.shape, x.dtype) for x in operands[1:]],
             pltpu.VMEM((2 * NF, time_dev), BF16),
-            pltpu.VMEM((KMAX * shots // 2, LANES), jnp.int32),
-            pltpu.SemaphoreType.DMA((6,)),
+            pltpu.SemaphoreType.DMA((3,)),
         ],
         compiler_params=params,
         cost_estimate=pl.CostEstimate(flops=2 * 16 * traces.size, bytes_accessed=2 * traces.size, transcendentals=0),
     )(*[pltpu.with_memory_space_constraint(x, pltpu.HBM) for x in operands])
     own = exchange(messages, 4)
     other = lax.ppermute(own, "freq", [(0, 1), (1, 0)])
+    counts, filtered = pl.pallas_call(
+        tables_kernel,
+        in_specs=[in_vmem()] * 4 + [pl.BlockSpec(memory_space=pl.ANY)],
+        out_specs=[in_vmem()] * 2,
+        out_shape=[
+            jax.ShapeDtypeStruct((shots, pairs), F32),
+            jax.ShapeDtypeStruct((shot_dev, 2 * NF, time_dev), BF16),
+        ],
+        scratch_shapes=[pltpu.VMEM((KMAX * shots // 2, LANES), jnp.int32)],
+        compiler_params=params,
+        cost_estimate=pl.CostEstimate(flops=1 << 22, bytes_accessed=1 << 19, transcendentals=0),
+    )(wide, filters, lengths, aperture.transpose(0, 2, 1), own)
 
     messages = pl.pallas_call(
         product_kernel,
@@ -313,6 +331,8 @@
             pltpu.VMEM((shots * 2 * NF, LANES), BF16),
             pltpu.VMEM((shots * 2 * NF, pairs), F32),
             pltpu.VMEM((2 * NF, pairs), F32),
+            pltpu.VMEM((shots * 2 * NF, LANES), F32),
+            pltpu.VMEM((shots * 2 * NF, LANES), F32),
         ],
         compiler_params=params,
         cost_estimate=pl.CostEstimate(flops=1 << 24, bytes_accessed=1 << 20, transcendentals=0),

time: 28.3 us -> 28 us (0.989)
  waiting for transfers between devices: 1.09 us -> 0.37 us
  Pallas kernels: 5.41 us -> 5.8 us
    ppermute x1, waiting for transfers between devices: 1.09 us -> 0.37 us  [shards(): other = lax.ppermute(own, 'freq', [(0, 1), (1, 0)])]
    pallas_call x0 -> x1, Pallas kernels: none -> 0.71 us  [shards(): pl.pallas_call(tables_kernel, in_specs=[in_vmem()] * 4 + [pl.BlockSpec(me...]
  transfers between devices with their start and end apart: 1 -> 1, of which waited for: 1 -> 1; matrix products, arithmetic and copies ran while one was open for 0% -> 0% of each run, Pallas kernels for 0% -> 3%
where the time goes in v7:
time: 28 us; the launch traced here: 27.6 us
  blocking collectives  21.2 us (76%)
  Pallas kernels  5.8 us (21%)
  waiting for transfers between devices  0.37 us (1%)
    all_to_all x2, blocking collectives, exchange(): lax.all_to_all(messages, DEVICES, split_axis=0, concat_axis=0, tiled=True...  21.2 us
    pallas_call x1, Pallas kernels, shards(): pl.pallas_call(analysis_kernel, in_specs=[in_hbm()] * len(operands), out_...  2.24 us
    pallas_call x1, Pallas kernels, shards(): pl.pallas_call(synthesis_kernel, in_specs=[in_vmem(), in_vmem()], out_spe...  1.75 us
    pallas_call x1, Pallas kernels, shards(): pl.pallas_call(product_kernel, in_specs=[in_vmem()] * 4, out_specs=in_vme...  1.1 us
    pallas_call x1, Pallas kernels, shards(): pl.pallas_call(tables_kernel, in_specs=[in_vmem()] * 4 + [pl.BlockSpec(me...  0.71 us
  transfers between devices with their start and end apart: 1, of which 1 were waited for; matrix products, arithmetic and copies ran while one was open for 0% of the time, Pallas kernels for 3%

profile of v7, /device:TPU:0, one launch (start us, length us, event | category | flops | bytes accessed | tf_op | source)
XLA Modules:
  0.0 27.6 jit_solution(12741368125560671915)
XLA Ops:
  0.0 0.0 copy-start.2
  0.0 0.0 copy-start.1
  0.0 0.0 copy-start
  0.0 2.2 %shard_map.55 = (bf16[16,24,128]{2,1,0:T(8,128)(2,1)S(1)}, bf16[128,2048]{1,0:T(8,128)(2,1)S(1)}, bf16[16,640]{1,0:T(8,128)(2,1)S(1)}) custom-call(s32[8]{0:T(128)} %bins_hbm.1, bf16[2,1024,512]{2,1,0:T(8,128)(2,1)} %traces_hbm.1), custom_call_target="tpu_custom_call" | custom-call | flops 33554432 | bytes 2097152 | tf_op jit(solution)/shard_map/pallas_call | solution.py:292
  2.3 12.2 %all_to_all.10._.own_ref = bf16[16,24,128]{2,1,0:T(8,128)(2,1)S(1)} all-to-all(bf16[16,24,128]{2,1,0:T(8,128)(2,1)S(1)} %get-tuple-element.10), channel_id=1, replica_groups={{22,0,2,4,6,9,11,13,15,16,18,20,25,27,29,31},{23,1,3,5,7,8,10,12,14,17,..., dimensions={0} | all-to-all | bytes 196608 | tf_op jit(solution)/shard_map/all_to_all | solution.py:280
  14.5 0.2 collective-permute-start
  14.7 0.0 copy-done.2
  14.7 0.0 copy-done.1
  14.7 0.0 copy-done
  14.7 0.7 %shard_map.56 = (f32[32,2048]{1,0:T(8,128)S(1)}, bf16[2,16,512]{2,1,0:T(8,128)(2,1)S(1)}) custom-call(bf16[16,640]{1,0:T(8,128)(2,1)S(1)} %get-tuple-element.11.wide_ref, bf16[2,31]{1,0:T(2,128)(2,1)S(1)} %copy-done.2, s32[32,64]{1,0:T(8,128)S(1)} %copy-done.1, s32[32,32,64]{2,1,0:T(8,128)S(1)} %bitcast.1, bf16[16,24,128]{2,1,0:T(8,128)(2,1)S(1)} %all_to_all.10._.own_ref), custom_call_target="tpu_custom_call" | custom-call | flops 4194304 | bytes 524288 | tf_op jit(solution)/shard_map/pallas_call | solution.py:312
  15.4 0.4 %collective-permute-done.other_ref = bf16[16,24,128]{2,1,0:T(8,128)(2,1)S(1)} collective-permute-done((bf16[16,24,128]{2,1,0:T(8,128)(2,1)S(1)}, bf16[16,24,128]{2,1,0:T(8,128)(2,1)S(1)}, u32[]{:S(2)}, u32[]{:S(2)}) %collective-permute-start) | collective-permute-done | bytes 98336 | tf_op jit(solution)/shard_map/ppermute | solution.py:311
  15.8 1.1 %shard_map.57 = bf16[16,16,128]{2,1,0:T(8,128)(2,1)S(1)} custom-call(bf16[16,24,128]{2,1,0:T(8,128)(2,1)S(1)} %all_to_all.10._.own_ref, bf16[16,24,128]{2,1,0:T(8,128)(2,1)S(1)} %collective-permute-done.other_ref, f32[32,2048]{1,0:T(8,128)S(1)} %get-tuple-element.12.counts_ref, bf16[128,2048]{1,0:T(8,128)(2,1)S(1)} %get-tuple-element.13.spread_ref), custom_call_target="tpu_custom_call" | custom-call | flops 16777216 | bytes 1048576 | tf_op jit(solution)/shard_map/pallas_call | solution.py:325
  16.9 8.9 %all_to_all.11.received_ref = bf16[16,16,128]{2,1,0:T(8,128)(2,1)S(1)} all-to-all(bf16[16,16,128]{2,1,0:T(8,128)(2,1)S(1)} %shard_map.57), channel_id=1, replica_groups={{23,0,2,4,6,8,10,12,14,17,19,21,25,27,29,31},{22,1,3,5,7,9,11,13,15,16,..., dimensions={0} | all-to-all | bytes 131072 | tf_op jit(solution)/shard_map/all_to_all | solution.py:280
  25.8 1.8 %shard_map.58 = bf16[2,1024,512]{2,1,0:T(8,128)(2,1)} custom-call(bf16[16,16,128]{2,1,0:T(8,128)(2,1)S(1)} %all_to_all.11.received_ref, bf16[2,16,512]{2,1,0:T(8,128)(2,1)S(1)} %get-tuple-element.14.filtered_ref), custom_call_target="tpu_custom_call" | custom-call | flops 33554432 | bytes 2097152 | tf_op jit(solution)/shard_map/pallas_call | solution.py:342
Async XLA Ops:
  0.0 14.7 %copy-start.2 = (bf16[2,31]{1,0:T(2,128)(2,1)S(1)}, bf16[2,31]{1,0:T(2,128)(2,1)}, u32[]{:S(2)}) copy-start(bf16[2,31]{1,0:T(2,128)(2,1)} %filters_ref.1) | copy-start | bytes 376
  0.0 14.7 %copy-start.1 = (s32[32,64]{1,0:T(8,128)S(1)}, s32[32,64]{1,0:T(8,128)}, u32[]{:S(2)}) copy-start(s32[32,64]{1,0:T(8,128)} %lengths_ref.1) | copy-start | bytes 24580
  0.0 14.7 %copy-start = (s32[32,64,32]{1,2,0:T(8,128)S(1)}, s32[32,64,32]{1,2,0:T(8,128)}, u32[]{:S(2)}) copy-start(s32[32,64,32]{1,2,0:T(8,128)} %param.7) | copy-start | bytes 786436
  14.5 1.3 %collective-permute-start = (bf16[16,24,128]{2,1,0:T(8,128)(2,1)S(1)}, bf16[16,24,128]{2,1,0:T(8,128)(2,1)S(1)}, u32[]{:S(2)}, u32[]{:S(2)}) collective-permute-start(bf16[16,24,128]{2,1,0:T(8,128)(2,1)S(1)} %all_to_all.10._.own_ref), channel_id=1, source_target_pairs={{0,1},{1,0},{2,3},{3,2},{4,5},{5,4},{6,7},{7,6},{8,9},{9,8},{10,11... | collective-permute-start | bytes 294920 | tf_op jit(solution)/shard_map/ppermute | solution.py:311

commit v8 on v7

--- a/solution.py
+++ b/solution.py
@@ -16,7 +16,13 @@
 PIECE = 32
 DEVICES = ("shot", "freq")
 CHIPS = 16
-ORDER = [11] + [g for g in range(CHIPS) if g != 11]
+
+
+def hops(a, b):
+    return abs(a // 4 - b // 4) + (a // 2 % 2 != b // 2 % 2) + (a % 2 != b % 2)
+
+
+ORDER = sorted(range(CHIPS), key=lambda g: hops(11, g))
 PLACES = [ORDER.index(g) for g in range(CHIPS)]
 
 

time: 28 us -> 27.4 us (0.979)
  blocking collectives: 21.2 us -> 20.4 us
  starting transfers between devices: 0.21 us -> 0.49 us
    all_to_all x2, blocking collectives: 21.2 us -> 20.4 us  [exchange(): lax.all_to_all(messages, DEVICES, split_axis=0, concat_axis=0, tiled=True...]
where the time goes in v8:
time: 27.4 us; the launch traced here: 27 us
  blocking collectives  20.4 us (74%)
  Pallas kernels  5.81 us (21%)
  starting transfers between devices  0.49 us (2%)
    all_to_all x2, blocking collectives, exchange(): lax.all_to_all(messages, DEVICES, split_axis=0, concat_axis=0, tiled=True...  20.4 us
    pallas_call x1, Pallas kernels, shards(): pl.pallas_call(analysis_kernel, in_specs=[in_hbm()] * len(operands), out_...  2.24 us
    pallas_call x1, Pallas kernels, shards(): pl.pallas_call(synthesis_kernel, in_specs=[in_vmem(), in_vmem()], out_spe...  1.76 us
    pallas_call x1, Pallas kernels, shards(): pl.pallas_call(product_kernel, in_specs=[in_vmem()] * 4, out_specs=in_vme...  1.1 us
    pallas_call x1, Pallas kernels, shards(): pl.pallas_call(tables_kernel, in_specs=[in_vmem()] * 4 + [pl.BlockSpec(me...  0.71 us
  transfers between devices with their start and end apart: 1, of which 1 were waited for; matrix products, arithmetic and copies ran while one was open for 0% of the time, Pallas kernels for 3%

profile of v8, /device:TPU:0, one launch (start us, length us, event | category | flops | bytes accessed | tf_op | source)
XLA Modules:
  0.0 27.0 jit_solution(3121070206004006174)
XLA Ops:
  0.0 0.0 copy-start.2
  0.0 0.0 copy-start.1
  0.0 0.0 copy-start
  0.0 2.2 %shard_map.55 = (bf16[16,24,128]{2,1,0:T(8,128)(2,1)S(1)}, bf16[128,2048]{1,0:T(8,128)(2,1)S(1)}, bf16[16,640]{1,0:T(8,128)(2,1)S(1)}) custom-call(s32[8]{0:T(128)} %bins_hbm.1, bf16[2,1024,512]{2,1,0:T(8,128)(2,1)} %traces_hbm.1), custom_call_target="tpu_custom_call" | custom-call | flops 33554432 | bytes 2097152 | tf_op jit(solution)/shard_map/pallas_call | solution.py:298
  2.3 11.7 %all_to_all.10._.own_ref = bf16[16,24,128]{2,1,0:T(8,128)(2,1)S(1)} all-to-all(bf16[16,24,128]{2,1,0:T(8,128)(2,1)S(1)} %get-tuple-element.10), channel_id=1, replica_groups={{22,15,18,20,31,6,11,13,16,27,29,2,4,9,25,0},{23,14,19,21,30,7,10,12,17..., dimensions={0} | all-to-all | bytes 196608 | tf_op jit(solution)/shard_map/all_to_all | solution.py:286
  13.9 0.5 %collective-permute-start = (bf16[16,24,128]{2,1,0:T(8,128)(2,1)S(1)}, bf16[16,24,128]{2,1,0:T(8,128)(2,1)S(1)}, u32[]{:S(2)}, u32[]{:S(2)}) collective-permute-start(bf16[16,24,128]{2,1,0:T(8,128)(2,1)S(1)} %all_to_all.10._.own_ref), channel_id=1, source_target_pairs={{0,1},{1,0},{2,3},{3,2},{4,5},{5,4},{6,7},{7,6},{8,9},{9,8},{10,11... | collective-permute-start | bytes 294920 | tf_op jit(solution)/shard_map/ppermute | solution.py:317
  14.4 0.0 copy-done.2
  14.4 0.0 copy-done.1
  14.4 0.0 copy-done
  14.4 0.7 %shard_map.56 = (f32[32,2048]{1,0:T(8,128)S(1)}, bf16[2,16,512]{2,1,0:T(8,128)(2,1)S(1)}) custom-call(bf16[16,640]{1,0:T(8,128)(2,1)S(1)} %get-tuple-element.11.wide_ref, bf16[2,31]{1,0:T(2,128)(2,1)S(1)} %copy-done.2, s32[32,64]{1,0:T(8,128)S(1)} %copy-done.1, s32[32,32,64]{2,1,0:T(8,128)S(1)} %bitcast.1, bf16[16,24,128]{2,1,0:T(8,128)(2,1)S(1)} %all_to_all.10._.own_ref), custom_call_target="tpu_custom_call" | custom-call | flops 4194304 | bytes 524288 | tf_op jit(solution)/shard_map/pallas_call | solution.py:318
  15.2 0.2 collective-permute-done.other_ref
  15.4 1.1 %shard_map.57 = bf16[16,16,128]{2,1,0:T(8,128)(2,1)S(1)} custom-call(bf16[16,24,128]{2,1,0:T(8,128)(2,1)S(1)} %all_to_all.10._.own_ref, bf16[16,24,128]{2,1,0:T(8,128)(2,1)S(1)} %collective-permute-done.other_ref, f32[32,2048]{1,0:T(8,128)S(1)} %get-tuple-element.12.counts_ref, bf16[128,2048]{1,0:T(8,128)(2,1)S(1)} %get-tuple-element.13.spread_ref), custom_call_target="tpu_custom_call" | custom-call | flops 16777216 | bytes 1048576 | tf_op jit(solution)/shard_map/pallas_call | solution.py:331
  16.5 8.7 %all_to_all.11.received_ref = bf16[16,16,128]{2,1,0:T(8,128)(2,1)S(1)} all-to-all(bf16[16,16,128]{2,1,0:T(8,128)(2,1)S(1)} %shard_map.57), channel_id=1, replica_groups={{23,14,19,21,31,6,10,12,17,27,29,2,4,8,25,0},{22,15,18,20,30,7,11,13,16..., dimensions={0} | all-to-all | bytes 131072 | tf_op jit(solution)/shard_map/all_to_all | solution.py:286
  25.2 1.8 %shard_map.58 = bf16[2,1024,512]{2,1,0:T(8,128)(2,1)} custom-call(bf16[16,16,128]{2,1,0:T(8,128)(2,1)S(1)} %all_to_all.11.received_ref, bf16[2,16,512]{2,1,0:T(8,128)(2,1)S(1)} %get-tuple-element.14.filtered_ref), custom_call_target="tpu_custom_call" | custom-call | flops 33554432 | bytes 2097152 | tf_op jit(solution)/shard_map/pallas_call | solution.py:348
Async XLA Ops:
  0.0 14.4 %copy-start.2 = (bf16[2,31]{1,0:T(2,128)(2,1)S(1)}, bf16[2,31]{1,0:T(2,128)(2,1)}, u32[]{:S(2)}) copy-start(bf16[2,31]{1,0:T(2,128)(2,1)} %filters_ref.1) | copy-start | bytes 376
  0.0 14.4 %copy-start.1 = (s32[32,64]{1,0:T(8,128)S(1)}, s32[32,64]{1,0:T(8,128)}, u32[]{:S(2)}) copy-start(s32[32,64]{1,0:T(8,128)} %lengths_ref.1) | copy-start | bytes 24580
  0.0 14.4 %copy-start = (s32[32,64,32]{1,2,0:T(8,128)S(1)}, s32[32,64,32]{1,2,0:T(8,128)}, u32[]{:S(2)}) copy-start(s32[32,64,32]{1,2,0:T(8,128)} %param.7) | copy-start | bytes 786436
  13.9 1.4 %collective-permute-start = (bf16[16,24,128]{2,1,0:T(8,128)(2,1)S(1)}, bf16[16,24,128]{2,1,0:T(8,128)(2,1)S(1)}, u32[]{:S(2)}, u32[]{:S(2)}) collective-permute-start(bf16[16,24,128]{2,1,0:T(8,128)(2,1)S(1)} %all_to_all.10._.own_ref), channel_id=1, source_target_pairs={{0,1},{1,0},{2,3},{3,2},{4,5},{5,4},{6,7},{7,6},{8,9},{9,8},{10,11... | collective-permute-start | bytes 294920 | tf_op jit(solution)/shard_map/ppermute | solution.py:317

commit v9 on v8

--- a/solution.py
+++ b/solution.py
@@ -257,7 +257,7 @@
     low = lax.broadcasted_iota(jnp.int32, (2 * NF, LANES), 1) < LANES // 2
     copies = []
     for tile in range(out_ref.shape[1] // LANES):
-        left, right = [received_ref[PLACES[2 * tile + i]].astype(F32) for i in range(2)]
+        left, right = [received_ref[PLACES[2 * tile + i]] for i in range(2)]
         spectra = (
             jnp.where(low, left, pltpu.roll(right, LANES // 2, 1)),
             jnp.where(low, pltpu.roll(left, LANES // 2, 1), right),
@@ -265,7 +265,7 @@
         rows = pl.ds(tile * LANES, LANES)
         for s in range(2):
             out_ref[s, rows, :] = lax.dot_general(
-                spectra[s].astype(BF16), filtered_ref[s], (((0,), (0,)), ((), ())), preferred_element_type=F32
+                spectra[s], filtered_ref[s], (((0,), (0,)), ((), ())), preferred_element_type=F32
             ).astype(BF16)
             copy = pltpu.make_async_copy(out_ref.at[s, rows, :], out_hbm.at[s, rows, :], out_sem.at[2 * tile + s])
             copy.start()

time: 27.4 us -> 27.4 us (level)
  no operation moved by 1% of the time
where the time goes in v9:
time: 27.4 us; the launch traced here: 27 us
  blocking collectives  20.4 us (74%)
  Pallas kernels  5.81 us (21%)
  starting transfers between devices  0.49 us (2%)
    all_to_all x2, blocking collectives, exchange(): lax.all_to_all(messages, DEVICES, split_axis=0, concat_axis=0, tiled=True...  20.4 us
    pallas_call x1, Pallas kernels, shards(): pl.pallas_call(analysis_kernel, in_specs=[in_hbm()] * len(operands), out_...  2.24 us
    pallas_call x1, Pallas kernels, shards(): pl.pallas_call(synthesis_kernel, in_specs=[in_vmem(), in_vmem()], out_spe...  1.76 us
    pallas_call x1, Pallas kernels, shards(): pl.pallas_call(product_kernel, in_specs=[in_vmem()] * 4, out_specs=in_vme...  1.1 us
    pallas_call x1, Pallas kernels, shards(): pl.pallas_call(tables_kernel, in_specs=[in_vmem()] * 4 + [pl.BlockSpec(me...  0.71 us
  transfers between devices with their start and end apart: 1, of which 1 were waited for; matrix products, arithmetic and copies ran while one was open for 0% of the time, Pallas kernels for 3%

profile of v9, /device:TPU:0, one launch (start us, length us, event | category | flops | bytes accessed | tf_op | source)
XLA Modules:
  0.0 27.0 jit_solution(6987809060445121719)
XLA Ops:
  0.0 0.0 copy-start.2
  0.0 0.0 copy-start.1
  0.0 0.0 copy-start
  0.0 2.2 %shard_map.55 = (bf16[16,24,128]{2,1,0:T(8,128)(2,1)S(1)}, bf16[128,2048]{1,0:T(8,128)(2,1)S(1)}, bf16[16,640]{1,0:T(8,128)(2,1)S(1)}) custom-call(s32[8]{0:T(128)} %bins_hbm.1, bf16[2,1024,512]{2,1,0:T(8,128)(2,1)} %traces_hbm.1), custom_call_target="tpu_custom_call" | custom-call | flops 33554432 | bytes 2097152 | tf_op jit(solution)/shard_map/pallas_call | solution.py:298
  2.3 11.7 %all_to_all.10._.own_ref = bf16[16,24,128]{2,1,0:T(8,128)(2,1)S(1)} all-to-all(bf16[16,24,128]{2,1,0:T(8,128)(2,1)S(1)} %get-tuple-element.10), channel_id=1, replica_groups={{22,15,18,20,31,6,11,13,16,27,29,2,4,9,25,0},{23,14,19,21,30,7,10,12,17..., dimensions={0} | all-to-all | bytes 196608 | tf_op jit(solution)/shard_map/all_to_all | solution.py:286
  13.9 0.5 %collective-permute-start = (bf16[16,24,128]{2,1,0:T(8,128)(2,1)S(1)}, bf16[16,24,128]{2,1,0:T(8,128)(2,1)S(1)}, u32[]{:S(2)}, u32[]{:S(2)}) collective-permute-start(bf16[16,24,128]{2,1,0:T(8,128)(2,1)S(1)} %all_to_all.10._.own_ref), channel_id=1, source_target_pairs={{0,1},{1,0},{2,3},{3,2},{4,5},{5,4},{6,7},{7,6},{8,9},{9,8},{10,11... | collective-permute-start | bytes 294920 | tf_op jit(solution)/shard_map/ppermute | solution.py:317
  14.4 0.0 copy-done.2
  14.4 0.0 copy-done.1
  14.4 0.0 copy-done
  14.4 0.7 %shard_map.56 = (f32[32,2048]{1,0:T(8,128)S(1)}, bf16[2,16,512]{2,1,0:T(8,128)(2,1)S(1)}) custom-call(bf16[16,640]{1,0:T(8,128)(2,1)S(1)} %get-tuple-element.11.wide_ref, bf16[2,31]{1,0:T(2,128)(2,1)S(1)} %copy-done.2, s32[32,64]{1,0:T(8,128)S(1)} %copy-done.1, s32[32,32,64]{2,1,0:T(8,128)S(1)} %bitcast.1, bf16[16,24,128]{2,1,0:T(8,128)(2,1)S(1)} %all_to_all.10._.own_ref), custom_call_target="tpu_custom_call" | custom-call | flops 4194304 | bytes 524288 | tf_op jit(solution)/shard_map/pallas_call | solution.py:318
  15.2 0.2 collective-permute-done.other_ref
  15.4 1.1 %shard_map.57 = bf16[16,16,128]{2,1,0:T(8,128)(2,1)S(1)} custom-call(bf16[16,24,128]{2,1,0:T(8,128)(2,1)S(1)} %all_to_all.10._.own_ref, bf16[16,24,128]{2,1,0:T(8,128)(2,1)S(1)} %collective-permute-done.other_ref, f32[32,2048]{1,0:T(8,128)S(1)} %get-tuple-element.12.counts_ref, bf16[128,2048]{1,0:T(8,128)(2,1)S(1)} %get-tuple-element.13.spread_ref), custom_call_target="tpu_custom_call" | custom-call | flops 16777216 | bytes 1048576 | tf_op jit(solution)/shard_map/pallas_call | solution.py:331
  16.5 8.7 %all_to_all.11.received_ref = bf16[16,16,128]{2,1,0:T(8,128)(2,1)S(1)} all-to-all(bf16[16,16,128]{2,1,0:T(8,128)(2,1)S(1)} %shard_map.57), channel_id=1, replica_groups={{23,14,19,21,31,6,10,12,17,27,29,2,4,8,25,0},{22,15,18,20,30,7,11,13,16..., dimensions={0} | all-to-all | bytes 131072 | tf_op jit(solution)/shard_map/all_to_all | solution.py:286
  25.2 1.8 %shard_map.58 = bf16[2,1024,512]{2,1,0:T(8,128)(2,1)} custom-call(bf16[16,16,128]{2,1,0:T(8,128)(2,1)S(1)} %all_to_all.11.received_ref, bf16[2,16,512]{2,1,0:T(8,128)(2,1)S(1)} %get-tuple-element.14.filtered_ref), custom_call_target="tpu_custom_call" | custom-call | flops 33554432 | bytes 2097152 | tf_op jit(solution)/shard_map/pallas_call | solution.py:348
Async XLA Ops:
  0.0 14.4 %copy-start.2 = (bf16[2,31]{1,0:T(2,128)(2,1)S(1)}, bf16[2,31]{1,0:T(2,128)(2,1)}, u32[]{:S(2)}) copy-start(bf16[2,31]{1,0:T(2,128)(2,1)} %filters_ref.1) | copy-start | bytes 376
  0.0 14.4 %copy-start.1 = (s32[32,64]{1,0:T(8,128)S(1)}, s32[32,64]{1,0:T(8,128)}, u32[]{:S(2)}) copy-start(s32[32,64]{1,0:T(8,128)} %lengths_ref.1) | copy-start | bytes 24580
  0.0 14.4 %copy-start = (s32[32,64,32]{1,2,0:T(8,128)S(1)}, s32[32,64,32]{1,2,0:T(8,128)}, u32[]{:S(2)}) copy-start(s32[32,64,32]{1,2,0:T(8,128)} %param.7) | copy-start | bytes 786436
  13.9 1.4 %collective-permute-start = (bf16[16,24,128]{2,1,0:T(8,128)(2,1)S(1)}, bf16[16,24,128]{2,1,0:T(8,128)(2,1)S(1)}, u32[]{:S(2)}, u32[]{:S(2)}) collective-permute-start(bf16[16,24,128]{2,1,0:T(8,128)(2,1)S(1)} %all_to_all.10._.own_ref), channel_id=1, source_target_pairs={{0,1},{1,0},{2,3},{3,2},{4,5},{5,4},{6,7},{7,6},{8,9},{9,8},{10,11... | collective-permute-start | bytes 294920 | tf_op jit(solution)/shard_map/ppermute | solution.py:317

commit v10 on v9

--- a/solution.py
+++ b/solution.py
@@ -22,7 +22,7 @@
     return abs(a // 4 - b // 4) + (a // 2 % 2 != b // 2 % 2) + (a % 2 != b % 2)
 
 
-ORDER = sorted(range(CHIPS), key=lambda g: hops(11, g))
+ORDER = sorted(range(CHIPS), key=lambda g: (hops(11, g), -hops(CHIPS - 1, g)))
 PLACES = [ORDER.index(g) for g in range(CHIPS)]
 
 

time: 27.4 us -> 27.4 us (level)
  no operation moved by 1% of the time
where the time goes in v10:
time: 27.4 us; the launch traced here: 27 us
  blocking collectives  20.4 us (74%)
  Pallas kernels  5.81 us (21%)
  starting transfers between devices  0.49 us (2%)
    all_to_all x2, blocking collectives, exchange(): lax.all_to_all(messages, DEVICES, split_axis=0, concat_axis=0, tiled=True...  20.4 us
    pallas_call x1, Pallas kernels, shards(): pl.pallas_call(analysis_kernel, in_specs=[in_hbm()] * len(operands), out_...  2.24 us
    pallas_call x1, Pallas kernels, shards(): pl.pallas_call(synthesis_kernel, in_specs=[in_vmem(), in_vmem()], out_spe...  1.76 us
    pallas_call x1, Pallas kernels, shards(): pl.pallas_call(product_kernel, in_specs=[in_vmem()] * 4, out_specs=in_vme...  1.1 us
    pallas_call x1, Pallas kernels, shards(): pl.pallas_call(tables_kernel, in_specs=[in_vmem()] * 4 + [pl.BlockSpec(me...  0.71 us
  transfers between devices with their start and end apart: 1, of which 1 were waited for; matrix products, arithmetic and copies ran while one was open for 0% of the time, Pallas kernels for 3%

profile of v10, /device:TPU:0, one launch (start us, length us, event | category | flops | bytes accessed | tf_op | source)
XLA Modules:
  0.0 27.0 jit_solution(6987809060445121719)
XLA Ops:
  0.0 0.0 copy-start.2
  0.0 0.0 copy-start.1
  0.0 0.0 copy-start
  0.0 2.2 %shard_map.55 = (bf16[16,24,128]{2,1,0:T(8,128)(2,1)S(1)}, bf16[128,2048]{1,0:T(8,128)(2,1)S(1)}, bf16[16,640]{1,0:T(8,128)(2,1)S(1)}) custom-call(s32[8]{0:T(128)} %bins_hbm.1, bf16[2,1024,512]{2,1,0:T(8,128)(2,1)} %traces_hbm.1), custom_call_target="tpu_custom_call" | custom-call | flops 33554432 | bytes 2097152 | tf_op jit(solution)/shard_map/pallas_call | solution.py:298
  2.3 11.7 %all_to_all.10._.own_ref = bf16[16,24,128]{2,1,0:T(8,128)(2,1)S(1)} all-to-all(bf16[16,24,128]{2,1,0:T(8,128)(2,1)S(1)} %get-tuple-element.10), channel_id=1, replica_groups={{22,15,18,20,31,6,11,13,16,27,29,2,4,9,25,0},{23,14,19,21,30,7,10,12,17..., dimensions={0} | all-to-all | bytes 196608 | tf_op jit(solution)/shard_map/all_to_all | solution.py:286
  13.9 0.5 %collective-permute-start = (bf16[16,24,128]{2,1,0:T(8,128)(2,1)S(1)}, bf16[16,24,128]{2,1,0:T(8,128)(2,1)S(1)}, u32[]{:S(2)}, u32[]{:S(2)}) collective-permute-start(bf16[16,24,128]{2,1,0:T(8,128)(2,1)S(1)} %all_to_all.10._.own_ref), channel_id=1, source_target_pairs={{0,1},{1,0},{2,3},{3,2},{4,5},{5,4},{6,7},{7,6},{8,9},{9,8},{10,11... | collective-permute-start | bytes 294920 | tf_op jit(solution)/shard_map/ppermute | solution.py:317
  14.4 0.0 copy-done.2
  14.4 0.0 copy-done.1
  14.4 0.0 copy-done
  14.4 0.7 %shard_map.56 = (f32[32,2048]{1,0:T(8,128)S(1)}, bf16[2,16,512]{2,1,0:T(8,128)(2,1)S(1)}) custom-call(bf16[16,640]{1,0:T(8,128)(2,1)S(1)} %get-tuple-element.11.wide_ref, bf16[2,31]{1,0:T(2,128)(2,1)S(1)} %copy-done.2, s32[32,64]{1,0:T(8,128)S(1)} %copy-done.1, s32[32,32,64]{2,1,0:T(8,128)S(1)} %bitcast.1, bf16[16,24,128]{2,1,0:T(8,128)(2,1)S(1)} %all_to_all.10._.own_ref), custom_call_target="tpu_custom_call" | custom-call | flops 4194304 | bytes 524288 | tf_op jit(solution)/shard_map/pallas_call | solution.py:318
  15.2 0.2 collective-permute-done.other_ref
  15.4 1.1 %shard_map.57 = bf16[16,16,128]{2,1,0:T(8,128)(2,1)S(1)} custom-call(bf16[16,24,128]{2,1,0:T(8,128)(2,1)S(1)} %all_to_all.10._.own_ref, bf16[16,24,128]{2,1,0:T(8,128)(2,1)S(1)} %collective-permute-done.other_ref, f32[32,2048]{1,0:T(8,128)S(1)} %get-tuple-element.12.counts_ref, bf16[128,2048]{1,0:T(8,128)(2,1)S(1)} %get-tuple-element.13.spread_ref), custom_call_target="tpu_custom_call" | custom-call | flops 16777216 | bytes 1048576 | tf_op jit(solution)/shard_map/pallas_call | solution.py:331
  16.5 8.7 %all_to_all.11.received_ref = bf16[16,16,128]{2,1,0:T(8,128)(2,1)S(1)} all-to-all(bf16[16,16,128]{2,1,0:T(8,128)(2,1)S(1)} %shard_map.57), channel_id=1, replica_groups={{23,14,19,21,31,6,10,12,17,27,29,2,4,8,25,0},{22,15,18,20,30,7,11,13,16..., dimensions={0} | all-to-all | bytes 131072 | tf_op jit(solution)/shard_map/all_to_all | solution.py:286
  25.2 1.8 %shard_map.58 = bf16[2,1024,512]{2,1,0:T(8,128)(2,1)} custom-call(bf16[16,16,128]{2,1,0:T(8,128)(2,1)S(1)} %all_to_all.11.received_ref, bf16[2,16,512]{2,1,0:T(8,128)(2,1)S(1)} %get-tuple-element.14.filtered_ref), custom_call_target="tpu_custom_call" | custom-call | flops 33554432 | bytes 2097152 | tf_op jit(solution)/shard_map/pallas_call | solution.py:348
Async XLA Ops:
  0.0 14.4 %copy-start.2 = (bf16[2,31]{1,0:T(2,128)(2,1)S(1)}, bf16[2,31]{1,0:T(2,128)(2,1)}, u32[]{:S(2)}) copy-start(bf16[2,31]{1,0:T(2,128)(2,1)} %filters_ref.1) | copy-start | bytes 376
  0.0 14.4 %copy-start.1 = (s32[32,64]{1,0:T(8,128)S(1)}, s32[32,64]{1,0:T(8,128)}, u32[]{:S(2)}) copy-start(s32[32,64]{1,0:T(8,128)} %lengths_ref.1) | copy-start | bytes 24580
  0.0 14.4 %copy-start = (s32[32,64,32]{1,2,0:T(8,128)S(1)}, s32[32,64,32]{1,2,0:T(8,128)}, u32[]{:S(2)}) copy-start(s32[32,64,32]{1,2,0:T(8,128)} %param.7) | copy-start | bytes 786436
  13.9 1.4 %collective-permute-start = (bf16[16,24,128]{2,1,0:T(8,128)(2,1)S(1)}, bf16[16,24,128]{2,1,0:T(8,128)(2,1)S(1)}, u32[]{:S(2)}, u32[]{:S(2)}) collective-permute-start(bf16[16,24,128]{2,1,0:T(8,128)(2,1)S(1)} %all_to_all.10._.own_ref), channel_id=1, source_target_pairs={{0,1},{1,0},{2,3},{3,2},{4,5},{5,4},{6,7},{7,6},{8,9},{9,8},{10,11... | collective-permute-start | bytes 294920 | tf_op jit(solution)/shard_map/ppermute | solution.py:317

commit v11 on v10

--- a/solution.py
+++ b/solution.py
@@ -213,9 +213,9 @@
     low = lax.broadcasted_iota(jnp.int32, (NF, LANES), 1) < LANES // 2
     for g in range(groups):
         place = PLACES[g]
-        rounded = (own_ref[place].astype(F32) + other_ref[place].astype(F32)).astype(BF16).astype(F32)
-        second_ref[:, g * LANES : (g + 1) * LANES] = rounded[: 2 * NF]
-        stations = rounded[2 * NF :]
+        spectra = own_ref[place].astype(F32) + other_ref[place].astype(F32)
+        second_ref[:, g * LANES : (g + 1) * LANES] = spectra[: 2 * NF]
+        stations = spectra[2 * NF :]
         for s in range(2):
             real = stations if s == 0 else pltpu.roll(stations, LANES - 8, 1)
             imag = pltpu.roll(stations, LANES - 16 - 8 * s, 1)

time: 27.4 us -> 27.4 us (level)
  no operation moved by 1% of the time
where the time goes in v11:
time: 27.4 us; the launch traced here: 27 us
  blocking collectives  20.4 us (74%)
  Pallas kernels  5.82 us (21%)
  starting transfers between devices  0.49 us (2%)
    all_to_all x2, blocking collectives, exchange(): lax.all_to_all(messages, DEVICES, split_axis=0, concat_axis=0, tiled=True...  20.4 us
    pallas_call x1, Pallas kernels, shards(): pl.pallas_call(analysis_kernel, in_specs=[in_hbm()] * len(operands), out_...  2.24 us
    pallas_call x1, Pallas kernels, shards(): pl.pallas_call(synthesis_kernel, in_specs=[in_vmem(), in_vmem()], out_spe...  1.76 us
    pallas_call x1, Pallas kernels, shards(): pl.pallas_call(product_kernel, in_specs=[in_vmem()] * 4, out_specs=in_vme...  1.11 us
    pallas_call x1, Pallas kernels, shards(): pl.pallas_call(tables_kernel, in_specs=[in_vmem()] * 4 + [pl.BlockSpec(me...  0.71 us
  transfers between devices with their start and end apart: 1, of which 1 were waited for; matrix products, arithmetic and copies ran while one was open for 0% of the time, Pallas kernels for 3%

profile of v11, /device:TPU:0, one launch (start us, length us, event | category | flops | bytes accessed | tf_op | source)
XLA Modules:
  0.0 27.0 jit_solution(3522264157698942114)
XLA Ops:
  0.0 0.0 copy-start.2
  0.0 0.0 copy-start.1
  0.0 0.0 copy-start
  0.0 2.2 %shard_map.55 = (bf16[16,24,128]{2,1,0:T(8,128)(2,1)S(1)}, bf16[128,2048]{1,0:T(8,128)(2,1)S(1)}, bf16[16,640]{1,0:T(8,128)(2,1)S(1)}) custom-call(s32[8]{0:T(128)} %bins_hbm.1, bf16[2,1024,512]{2,1,0:T(8,128)(2,1)} %traces_hbm.1), custom_call_target="tpu_custom_call" | custom-call | flops 33554432 | bytes 2097152 | tf_op jit(solution)/shard_map/pallas_call | solution.py:298
  2.3 11.7 %all_to_all.10._.own_ref = bf16[16,24,128]{2,1,0:T(8,128)(2,1)S(1)} all-to-all(bf16[16,24,128]{2,1,0:T(8,128)(2,1)S(1)} %get-tuple-element.10), channel_id=1, replica_groups={{22,15,18,20,31,6,11,13,16,27,29,2,4,9,25,0},{23,14,19,21,30,7,10,12,17..., dimensions={0} | all-to-all | bytes 196608 | tf_op jit(solution)/shard_map/all_to_all | solution.py:286
  13.9 0.5 %collective-permute-start = (bf16[16,24,128]{2,1,0:T(8,128)(2,1)S(1)}, bf16[16,24,128]{2,1,0:T(8,128)(2,1)S(1)}, u32[]{:S(2)}, u32[]{:S(2)}) collective-permute-start(bf16[16,24,128]{2,1,0:T(8,128)(2,1)S(1)} %all_to_all.10._.own_ref), channel_id=1, source_target_pairs={{0,1},{1,0},{2,3},{3,2},{4,5},{5,4},{6,7},{7,6},{8,9},{9,8},{10,11... | collective-permute-start | bytes 294920 | tf_op jit(solution)/shard_map/ppermute | solution.py:317
  14.4 0.0 copy-done.2
  14.4 0.0 copy-done.1
  14.4 0.0 copy-done
  14.4 0.7 %shard_map.56 = (f32[32,2048]{1,0:T(8,128)S(1)}, bf16[2,16,512]{2,1,0:T(8,128)(2,1)S(1)}) custom-call(bf16[16,640]{1,0:T(8,128)(2,1)S(1)} %get-tuple-element.11.wide_ref, bf16[2,31]{1,0:T(2,128)(2,1)S(1)} %copy-done.2, s32[32,64]{1,0:T(8,128)S(1)} %copy-done.1, s32[32,32,64]{2,1,0:T(8,128)S(1)} %bitcast.1, bf16[16,24,128]{2,1,0:T(8,128)(2,1)S(1)} %all_to_all.10._.own_ref), custom_call_target="tpu_custom_call" | custom-call | flops 4194304 | bytes 524288 | tf_op jit(solution)/shard_map/pallas_call | solution.py:318
  15.2 0.2 collective-permute-done.other_ref
  15.4 1.1 %shard_map.57 = bf16[16,16,128]{2,1,0:T(8,128)(2,1)S(1)} custom-call(bf16[16,24,128]{2,1,0:T(8,128)(2,1)S(1)} %all_to_all.10._.own_ref, bf16[16,24,128]{2,1,0:T(8,128)(2,1)S(1)} %collective-permute-done.other_ref, f32[32,2048]{1,0:T(8,128)S(1)} %get-tuple-element.12.counts_ref, bf16[128,2048]{1,0:T(8,128)(2,1)S(1)} %get-tuple-element.13.spread_ref), custom_call_target="tpu_custom_call" | custom-call | flops 16777216 | bytes 1048576 | tf_op jit(solution)/shard_map/pallas_call | solution.py:331
  16.5 8.7 %all_to_all.11.received_ref = bf16[16,16,128]{2,1,0:T(8,128)(2,1)S(1)} all-to-all(bf16[16,16,128]{2,1,0:T(8,128)(2,1)S(1)} %shard_map.57), channel_id=1, replica_groups={{23,14,19,21,31,6,10,12,17,27,29,2,4,8,25,0},{22,15,18,20,30,7,11,13,16..., dimensions={0} | all-to-all | bytes 131072 | tf_op jit(solution)/shard_map/all_to_all | solution.py:286
  25.2 1.8 %shard_map.58 = bf16[2,1024,512]{2,1,0:T(8,128)(2,1)} custom-call(bf16[16,16,128]{2,1,0:T(8,128)(2,1)S(1)} %all_to_all.11.received_ref, bf16[2,16,512]{2,1,0:T(8,128)(2,1)S(1)} %get-tuple-element.14.filtered_ref), custom_call_target="tpu_custom_call" | custom-call | flops 33554432 | bytes 2097152 | tf_op jit(solution)/shard_map/pallas_call | solution.py:348
Async XLA Ops:
  0.0 14.4 %copy-start.2 = (bf16[2,31]{1,0:T(2,128)(2,1)S(1)}, bf16[2,31]{1,0:T(2,128)(2,1)}, u32[]{:S(2)}) copy-start(bf16[2,31]{1,0:T(2,128)(2,1)} %filters_ref.1) | copy-start | bytes 376
  0.0 14.4 %copy-start.1 = (s32[32,64]{1,0:T(8,128)S(1)}, s32[32,64]{1,0:T(8,128)}, u32[]{:S(2)}) copy-start(s32[32,64]{1,0:T(8,128)} %lengths_ref.1) | copy-start | bytes 24580
  0.0 14.4 %copy-start = (s32[32,64,32]{1,2,0:T(8,128)S(1)}, s32[32,64,32]{1,2,0:T(8,128)}, u32[]{:S(2)}) copy-start(s32[32,64,32]{1,2,0:T(8,128)} %param.7) | copy-start | bytes 786436
  13.9 1.4 %collective-permute-start = (bf16[16,24,128]{2,1,0:T(8,128)(2,1)S(1)}, bf16[16,24,128]{2,1,0:T(8,128)(2,1)S(1)}, u32[]{:S(2)}, u32[]{:S(2)}) collective-permute-start(bf16[16,24,128]{2,1,0:T(8,128)(2,1)S(1)} %all_to_all.10._.own_ref), channel_id=1, source_target_pairs={{0,1},{1,0},{2,3},{3,2},{4,5},{5,4},{6,7},{7,6},{8,9},{9,8},{10,11... | collective-permute-start | bytes 294920 | tf_op jit(solution)/shard_map/ppermute | solution.py:317
